TPU v7x, 32 devices: a whole 2x2x4 slice. The times are simulated.
32 devices in a mesh: batch: 4 (over y, x), blk: 8 (over z, core).
Axes of the slice: x: 2, y: 2, z: 4, core: 2. Of those that a mesh axis runs over, the one named last changes fastest.
Arguments:
- tokens: bfloat16 [32, 1024, 1024], P('batch', 'blk'), may hold values from -6 to 6
- lengths: int32 [32], P('batch'), may hold values from 64 to 1024, as said below
- norm_gain: bfloat16 [1024], replicated, may hold values from 0.5 to 1.5
- norm_shift: bfloat16 [1024], replicated, may hold values from -1.25 to 1.25
- joint_weight: bfloat16 [1024, 3072], replicated, may hold values from -0.1875 to 0.1875
- query_bias: bfloat16 [1024], replicated, may hold values from -1.25 to 1.25
- value_bias: bfloat16 [1024], replicated, may hold values from -1.25 to 1.25
- output_weight: bfloat16 [1024, 1024], replicated, may hold values from -0.75 to 0.75
- output_bias: bfloat16 [1024], replicated, may hold values from -1.25 to 1.25
- second_gain: bfloat16 [1024], replicated, may hold values from 0.5 to 1.5
- second_shift: bfloat16 [1024], replicated, may hold values from -1.25 to 1.25
- upward_weight: bfloat16 [1024, 4096], replicated, may hold values from -0.1875 to 0.1875
- upward_bias: bfloat16 [4096], replicated, may hold values from -1.25 to 1.25
- down_weight: bfloat16 [4096, 1024], replicated, may hold values from -0.09375 to 0.09375
- down_bias: bfloat16 [1024], replicated, may hold values from -1.25 to 1.25
- query_down: bfloat16 [1024, 4], replicated, may hold values from -0.1875 to 0.1875
- query_up: bfloat16 [4, 1024], replicated, may hold values from -0.1875 to 0.1875
- value_down: bfloat16 [1024, 4], replicated, may hold values from -0.1875 to 0.1875
- value_up: bfloat16 [4, 1024], replicated, may hold values from -0.1875 to 0.1875
- cotangent: bfloat16 [32, 1024, 1024], P('batch', 'blk'), may hold values from -6 to 6
Outputs:
- block_output: bfloat16 [32, 1024, 1024], P('batch', 'blk')
- token_grads: float32 [32, 1024, 1024], P('batch', 'blk')
- query_down_grad: float32 [1024, 4], replicated
- query_up_grad: float32 [4, 1024], replicated
- value_down_grad: float32 [1024, 4], replicated
- value_up_grad: float32 [4, 1024], replicated
Inputs may be any that keep to these rules, and one draw needn't show every extreme that they name: `lengths`: in each group of 8 slots of one index of batch, one slot drawn from the seed has length 1024.
All inputs are finite; a program needn't handle non-finite values.
Results may differ from a plain program's by a relative error of at most 0.015.
Values may be sent and summed in bfloat16 or wider, within the bound.
No kernel may reach another device: no remote copies, remote signals or barrier semaphores. Data moves between devices by JAX's collectives and lax.ppermute only.
A program may use at most 320 MiB of HBM per device.

v0:
```python
from functools import partial

import jax
import jax.numpy as jnp
from jax import lax
from jax.sharding import PartitionSpec as P

HD = 64
RANK = 4


epsilon = 1e-05
masked_value = -1e30


def normalize(values, gain, shift):
    centred = values - jnp.mean(values, axis=-1, keepdims=True)
    inverse = lax.rsqrt(jnp.mean(centred * centred, axis=-1, keepdims=True) + epsilon)
    standard = centred * inverse
    return (standard * gain.astype(jnp.float32) + shift.astype(jnp.float32), standard, inverse)


def norm_back(grad, standard, inverse, gain):
    scaled = grad * gain.astype(jnp.float32)
    centred = scaled - jnp.mean(scaled, axis=-1, keepdims=True)
    return inverse * (centred - standard * jnp.mean(scaled * standard, axis=-1, keepdims=True))


def transposed(left, right):
    return lax.dot_general(
        left, right, (((0,), (0,)), ((), ())), preferred_element_type=jnp.float32
    )


def against(left, right):
    return lax.dot_general(
        left, right, (((1,), (1,)), ((), ())), preferred_element_type=jnp.float32
    )


def body(
    tokens,
    lengths,
    norm_gain,
    norm_shift,
    joint_weight,
    query_bias,
    value_bias,
    output_weight,
    output_bias,
    second_gain,
    second_shift,
    upward_weight,
    upward_bias,
    down_weight,
    down_bias,
    query_down,
    query_up,
    value_down,
    value_up,
    cotangent,
):
    seqs_here, rows, width = tokens.shape
    heads = width // HD
    positions = seqs_here * rows
    length_all = rows * lax.axis_size("blk")
    scale = HD ** (-0.5)
    adapter = 32.0 / RANK
    flat = tokens.reshape(positions, width).astype(jnp.float32)
    normed_full, standard, inverse = normalize(flat, norm_gain, norm_shift)
    normed = normed_full.astype(jnp.bfloat16)
    joint = jnp.dot(normed, joint_weight, preferred_element_type=jnp.float32)
    query_low = jnp.dot(normed, query_down, preferred_element_type=jnp.float32).astype(jnp.bfloat16)
    value_low = jnp.dot(normed, value_down, preferred_element_type=jnp.float32).astype(jnp.bfloat16)
    queries = (
        joint[:, :width]
        + query_bias.astype(jnp.float32)
        + adapter * jnp.dot(query_low, query_up, preferred_element_type=jnp.float32)
    ).astype(jnp.bfloat16)
    keys_here = joint[:, width : 2 * width].astype(jnp.bfloat16)
    values_here = (
        joint[:, 2 * width :]
        + value_bias.astype(jnp.float32)
        + adapter * jnp.dot(value_low, value_up, preferred_element_type=jnp.float32)
    ).astype(jnp.bfloat16)
    query_heads = queries.reshape(seqs_here, rows, heads, HD)
    key_blocks = keys_here.reshape(seqs_here, rows, width)
    value_blocks = values_here.reshape(seqs_here, rows, width)
    device = lax.axis_index("blk")
    query_place = device * rows + jnp.arange(rows, dtype=jnp.int32)
    limits = lengths[:, None, None, None]

    def visible(query_pos, key_pos):
        return (key_pos[None, None, None, :] <= query_pos[None, None, :, None]) & (
            key_pos[None, None, None, :] < limits
        )

    running = jnp.full((seqs_here, heads, rows), masked_value, jnp.float32)
    key_piece = lax.all_gather(key_blocks, "blk", axis=1, tiled=True)
    value_piece = lax.all_gather(value_blocks, "blk", axis=1, tiled=True)
    count = key_piece.shape[1]
    key_heads = key_piece.reshape(seqs_here, count, heads, HD)
    value_heads = value_piece.reshape(seqs_here, count, heads, HD)
    allowed = visible(query_place, jnp.arange(count, dtype=jnp.int32))
    scores = (
        jnp.einsum("sqhd,skhd->shqk", query_heads, key_heads, preferred_element_type=jnp.float32)
        * scale
    )
    masked = jnp.where(allowed, scores, masked_value)
    highest = jnp.maximum(running, jnp.max(masked, axis=-1))
    weights = jnp.where(allowed, jnp.exp(masked - highest[..., None]), 0.0)
    totals = jnp.sum(weights, axis=-1)
    update = jnp.einsum(
        "shqk,skhd->sqhd",
        weights.astype(jnp.bfloat16),
        value_heads,
        preferred_element_type=jnp.float32,
    )
    summed = update
    running, totals, summed = (highest, totals, summed)
    mixed_full = summed / jnp.transpose(totals, (0, 2, 1))[..., None]
    log_total = running + jnp.log(totals)
    mixed_low = mixed_full.reshape(positions, width).astype(jnp.bfloat16)
    middle = (
        flat
        + jnp.dot(mixed_low, output_weight, preferred_element_type=jnp.float32)
        + output_bias.astype(jnp.float32)
    )
    normed_two_full, standard_two, inverse_two = normalize(middle, second_gain, second_shift)
    normed_two = normed_two_full.astype(jnp.bfloat16)
    hidden = jnp.dot(
        normed_two, upward_weight, preferred_element_type=jnp.float32
    ) + upward_bias.astype(jnp.float32)
    active_full, gelu_pull = jax.vjp(partial(jax.nn.gelu, approximate=True), hidden)
    active = active_full.astype(jnp.bfloat16)
    block_output = (
        (
            middle
            + jnp.dot(active, down_weight, preferred_element_type=jnp.float32)
            + down_bias.astype(jnp.float32)
        )
        .astype(jnp.bfloat16)
        .reshape(seqs_here, rows, width)
    )
    outer = cotangent.reshape(positions, width)
    d_active = against(outer, down_weight)
    d_hidden = gelu_pull(d_active)[0].astype(jnp.bfloat16)
    d_normed_two = against(d_hidden, upward_weight)
    d_middle = outer.astype(jnp.float32) + norm_back(
        d_normed_two, standard_two, inverse_two, second_gain
    )
    d_branch = d_middle.astype(jnp.bfloat16)
    d_mixed = against(d_branch, output_weight).astype(jnp.bfloat16)
    d_mixed_heads = d_mixed.reshape(seqs_here, rows, heads, HD)
    delta = jnp.transpose(
        jnp.sum(d_mixed_heads.astype(jnp.float32) * mixed_full, axis=-1), (0, 2, 1)
    )
    key_all, value_all = (
        lax.all_gather(key_blocks, "blk", axis=1, tiled=True),
        lax.all_gather(value_blocks, "blk", axis=1, tiled=True),
    )
    key_heads_all = key_all.reshape(seqs_here, length_all, heads, HD)
    value_heads_all = value_all.reshape(seqs_here, length_all, heads, HD)
    allowed_all = visible(query_place, jnp.arange(length_all, dtype=jnp.int32))
    scores = (
        jnp.einsum(
            "sqhd,skhd->shqk", query_heads, key_heads_all, preferred_element_type=jnp.float32
        )
        * scale
    )
    probs = jnp.where(allowed_all, jnp.exp(scores - log_total[..., None]), 0.0)
    d_probs = jnp.einsum(
        "sqhd,skhd->shqk", d_mixed_heads, value_heads_all, preferred_element_type=jnp.float32
    )
    d_scores = (probs * (d_probs - delta[..., None])).astype(jnp.bfloat16)
    d_queries = (
        jnp.einsum("shqk,skhd->sqhd", d_scores, key_heads_all, preferred_element_type=jnp.float32)
        * scale
    )
    d_keys_all = (
        jnp.einsum("shqk,sqhd->kshd", d_scores, query_heads, preferred_element_type=jnp.float32)
        * scale
    )
    d_values_all = jnp.einsum(
        "shqk,sqhd->kshd",
        probs.astype(jnp.bfloat16),
        d_mixed_heads,
        preferred_element_type=jnp.float32,
    )
    stacked = jnp.stack(
        (
            d_keys_all.reshape(length_all, seqs_here, width),
            d_values_all.reshape(length_all, seqs_here, width),
        ),
        axis=2,
    )
    owned = lax.psum_scatter(
        stacked.astype(jnp.bfloat16), "blk", scatter_dimension=0, tiled=True
    ).astype(jnp.float32)
    d_keys = jnp.transpose(owned[:, :, 0], (1, 0, 2)).reshape(positions, width)
    d_values = jnp.transpose(owned[:, :, 1], (1, 0, 2)).reshape(positions, width)
    d_query_low = d_queries.reshape(positions, width).astype(jnp.bfloat16)
    d_key_low = d_keys.astype(jnp.bfloat16)
    d_value_low = d_values.astype(jnp.bfloat16)
    query_up_grad = adapter * transposed(query_low, d_query_low)
    value_up_grad = adapter * transposed(value_low, d_value_low)
    d_query_small = (adapter * against(d_query_low, query_up)).astype(jnp.bfloat16)
    d_value_small = (adapter * against(d_value_low, value_up)).astype(jnp.bfloat16)
    query_down_grad = transposed(normed, d_query_small)
    value_down_grad = transposed(normed, d_value_small)
    d_joint = jnp.concatenate((d_query_low, d_key_low, d_value_low), axis=1)
    d_normed = (
        against(d_joint, joint_weight)
        + against(d_query_small, query_down)
        + against(d_value_small, value_down)
    )
    token_grads = (d_middle + norm_back(d_normed, standard, inverse, norm_gain)).reshape(
        seqs_here, rows, width
    )
    sums = lax.psum(
        (query_down_grad, query_up_grad, value_down_grad, value_up_grad), ("batch", "blk")
    )
    return (block_output, token_grads, sums[0], sums[1], sums[2], sums[3])


def solution(mesh):
    placed = (
        P("batch", "blk", None),
        P("batch"),
        P(),
        P(),
        P(),
        P(),
        P(),
        P(),
        P(),
        P(),
        P(),
        P(),
        P(),
        P(),
        P(),
        P(),
        P(),
        P(),
        P(),
        P("batch", "blk", None),
    )
    return jax.shard_map(
        body,
        mesh=mesh,
        in_specs=placed,
        out_specs=(P("batch", "blk", None), P("batch", "blk", None), P(), P(), P(), P()),
        check_vma=False,
    )
```

profile of v0, /device:TPU:0, one launch (start us, length us, event | category | flops | bytes accessed | tf_op | source)
XLA Modules:
  0.0 1101.9 jit_solution(5030795331936804348)
XLA Ops:
  15.0 6.7 fusion.91
  29.9 4.4 fusion.34
  38.1 4.9 fusion.32
  43.0 6.6 reshape.198
  49.7 5.8 copy.33
  56.2 124.7 %all-gather.5.cloned.1.call-done = bf16[8,1024,1024]{2,1,0:T(8,128)(2,1)} async-done(((bf16[8,128,1024]{2,1,0:T(8,128)(2,1)}), bf16[8,1024,1024]{2,1,0:T(8,128)(2,1)}) %all-gather.5.cloned.1.call-update) | async-done | bytes 16777232 | tf_op jit(solution)/shard_map/all_gather | solution.py:99
  180.8 22.3 %copy.32 = bf16[8,1024,1024]{1,2,0:T(8,128)(2,1)} copy(bf16[8,1024,1024]{2,1,0:T(8,128)(2,1)} %all-gather.5.cloned.1.call-done) | data formatting | bytes 33554432 | tf_op jit(solution)/shard_map/all_gather | solution.py:99
  203.1 32.1 %select_reduce_fusion = (f32[8,16,128]{2,1,0:T(8,128)S(1)}, f32[8,16,128,1024]{3,2,1,0:T(8,128)}) fusion(pred[8,128,1024]{2,1,0:T(8,128)(4,1)S(1)} %broadcast_and_fusion, bf16[8,128,16,64]{1,3,2,0:T(8,128)(2,1)} %copy.33, bf16[8,1024,16,64]{1,3,2,0:T(8,128)(2,1)} %bitcast.122), kind=kOutput, calls=%fused_computation.3 | convolution fusion | flops 2197798912 | bytes 87097344 | tf_op jit(solution)/shard_map/sqhd,skhd->shqk/dot_general | solution.py:106
  235.3 22.5 %fusion.1 = f32[8,16,128]{2,1,0:T(8,128)S(1)} fusion(f32[8,16,128,1024]{3,2,1,0:T(8,128)} %get-tuple-element.19, f32[8,16,128]{2,1,0:T(8,128)S(1)} %broadcast_maximum_fusion, pred[8,128,1024]{2,1,0:T(8,128)(4,1)S(1)} %broadcast_and_fusion), kind=kLoop, calls=%fused_computation.5 | loop fusion | flops 83869696 | bytes 68288512 | tf_op jit(solution)/shard_map/reduce_sum | solution.py:112
  258.4 73.4 %all-gather.3.cloned.1.call-done = bf16[8,1024,1024]{2,1,0:T(8,128)(2,1)} async-done(((bf16[8,128,1024]{2,1,0:T(8,128)(2,1)}), bf16[8,1024,1024]{2,1,0:T(8,128)(2,1)}) %all-gather.3.cloned.1.call-update) | async-done | bytes 16777232 | tf_op jit(solution)/shard_map/all_gather | solution.py:100
  331.8 21.6 %copy.30 = bf16[8,1024,1024]{1,2,0:T(8,128)(2,1)} copy(bf16[8,1024,1024]{2,1,0:T(8,128)(2,1)} %all-gather.3.cloned.1.call-done) | data formatting | bytes 33554432 | tf_op jit(solution)/shard_map/all_gather | solution.py:100
  353.3 32.1 %fusion.87 = (bf16[8,128,16,64]{1,3,2,0:T(8,128)(2,1)S(1)}, f32[8,128,16,64]{1,3,2,0:T(8,128)}) fusion(f32[8,128,16]{1,2,0:T(8,128)S(1)} %bitcast.141, bf16[8,1024,16,64]{1,3,2,0:T(8,128)(2,1)} %bitcast.131, f32[8,16,128,1024]{3,2,1,0:T(8,128)} %get-tuple-element.19, f32[8,16,128]{2,1,0:T(8,128)S(1)} %broadcast_maximum_fusion, ...), kind=kOutput, calls=%fused_computation.124 | convolution fusion | flops 2233466880 | bytes 91357184 | tf_op jit(solution)/shard_map/shqk,skhd->sqhd/dot_general | solution.py:113
  390.7 12.6 %fusion.50 = f32[1024,4096]{1,0:T(8,128)} fusion(bf16[1024,4096]{1,0:T(8,128)(2,1)S(1)} %bitcast.144, f32[1024,1024]{1,0:T(8,128)S(1)} %get-tuple-element.23, f32[1024]{0:T(1024)S(1)} %convert_element_type.148, f32[1024]{0:T(1024)S(1)} %convert_element_type.147, f32[1024]{0:T(1024)S(1)} %add_rsqrt_fusion, f32[1024]{0:T(1024)S(1)} %broadcast_multiply_fusion.4), kind=kOutput, calls=%fused_computation.70 | convolution fusion | flops 8595177472 | bytes 29376512 | tf_op jit(solution)/shard_map/dot_general | solution.py:131
  403.4 32.3 %multiply_reduce_fusion.3 = (f32[1024]{0:T(1024)S(1)}, f32[1024]{0:T(1024)S(1)}, f32[1024,1024]{1,0:T(8,128)}) fusion(f32[1024]{0:T(1024)S(1)} %convert_element_type.147, f32[1024]{0:T(1024)S(1)} %add_rsqrt_fusion, f32[1024,1024]{1,0:T(8,128)} %copy-done.9, f32[1024]{0:T(1024)S(1)} %broadcast_multiply_fusion.4, bf16[1024,4096]{1,0:T(8,128)(2,1)} %param.31, ...), kind=kOutput, calls=%fused_computation.69 | convolution fusion | flops 17274241024 | bytes 44077056 | tf_op jit(solution)/shard_map/dot_general | solution.py:36
  435.7 4.7 multiply_add_fusion
  446.3 6.3 reshape.199
  452.6 4.9 copy.36
  457.6 4.0 multiply_reduce_fusion
  461.6 30.5 %fusion.19 = bf16[8,16,64,1024]{3,2,1,0:T(8,128)(2,1)} fusion(bf16[8,128,16,64]{1,3,2,0:T(8,128)(2,1)S(1)} %copy.36, f32[8,16,128,1024]{3,2,1,0:T(8,128)} %get-tuple-element.19, f32[8,16,128]{2,1,0:T(8,128)S(1)} %copy-done.19, pred[8,128,1024]{2,1,0:T(8,128)(4,1)S(1)} %broadcast_and_fusion), kind=kOutput, calls=%fused_computation.26 | convolution fusion | flops 2222981120 | bytes 87097344 | tf_op jit(solution)/shard_map/shqk,sqhd->kshd/dot_general | solution.py:184
  492.1 43.5 %multiply_convert_fusion = bf16[8,16,128,1024]{3,2,1,0:T(8,128)(2,1)} fusion(f32[8,16,128,1024]{3,2,1,0:T(8,128)} %get-tuple-element.19, f32[8,16,128]{2,1,0:T(8,128)S(1)} %bitcast.142, f32[8,16,128]{2,1,0:T(8,128)S(1)} %copy-done.19, pred[8,128,1024]{2,1,0:T(8,128)(4,1)S(1)} %broadcast_and_fusion, bf16[8,128,16,64]{1,3,2,0:T(8,128)(2,1)} %copy-done.14, ...), kind=kOutput, calls=%fused_computation | convolution fusion | flops 2248146944 | bytes 120717312 | tf_op jit(solution)/shard_map/sqhd,skhd->shqk/dot_general | solution.py:172
  535.6 16.8 %multiply_convert_fusion.1 = bf16[8,16,64,1024]{3,2,1,0:T(8,128)(2,1)} fusion(bf16[8,128,16,64]{1,3,2,0:T(8,128)(2,1)S(1)} %copy-done.8, bf16[8,16,128,1024]{3,2,1,0:T(8,128)(2,1)} %multiply_convert_fusion), kind=kOutput, calls=%fused_computation.9 | convolution fusion | flops 2164260864 | bytes 52428800 | tf_op jit(solution)/shard_map/shqk,sqhd->kshd/dot_general | solution.py:181
  552.3 21.6 %copy.41 = bf16[1024,8,1,1024]{3,0,1,2:T(8,128)(2,1)} copy(bf16[1024,8,1,1024]{0,3,1,2:T(8,128)(2,1)} %bitcast.124) | data formatting | bytes 33554432 | tf_op jit(solution)/shard_map/stack;reshape | solution.py:190
  573.9 21.5 %copy.42 = bf16[1024,8,1,1024]{3,0,1,2:T(8,128)(2,1)} copy(bf16[1024,8,1,1024]{0,3,1,2:T(8,128)(2,1)} %bitcast.133) | data formatting | bytes 33554432 | tf_op jit(solution)/shard_map/stack;reshape | solution.py:190
  595.4 23.0 %pad_maximum_fusion = bf16[1024,8,2,1024]{3,0,1,2:T(8,128)(2,1)} fusion(bf16[1024,8,1,1024]{3,0,1,2:T(8,128)(2,1)} %copy.42, bf16[1024,8,1,1024]{3,0,1,2:T(8,128)(2,1)} %copy.41), kind=kLoop, calls=%fused_computation.8 | loop fusion | flops 16777216 | bytes 67108864 | tf_op jit(solution)/shard_map/stack | solution.py:190
  619.2 20.7 %fusion.65 = bf16[8,128,16,64]{1,3,2,0:T(8,128)(2,1)S(1)} fusion(bf16[8,1024,16,64]{1,3,2,0:T(8,128)(2,1)} %bitcast.123, bf16[8,16,128,1024]{3,2,1,0:T(8,128)(2,1)} %multiply_convert_fusion), kind=kOutput, calls=%fused_computation.83 | convolution fusion | flops 2149580800 | bytes 52428800 | tf_op jit(solution)/shard_map/shqk,skhd->sqhd/dot_general | solution.py:177
  649.1 17.9 %add_convert_fusion = bf16[1024,1024]{1,0:T(8,128)(2,1)} fusion(f32[1024,1024]{1,0:T(8,128)S(1)} %copy-done.10, f32[1024]{0:T(1024)S(1)} %convert_element_type.152, bf16[4096,1024]{1,0:T(8,128)(2,1)} %param.33, f32[1024,4096]{1,0:T(8,128)} %fusion.50, f32[4096]{0:T(1024)S(1)} %copy-done.33), kind=kOutput, calls=%fused_computation.65 | convolution fusion | flops 8635023360 | bytes 31477760 | tf_op jit(solution)/shard_map/dot_general | solution.py:139
  667.1 275.3 %reduce-scatter.2.cloned.1.call-done = bf16[128,8,2,1024]{3,0,1,2:T(8,128)(2,1)} async-done(((bf16[1024,8,2,1024]{3,0,1,2:T(8,128)(2,1)}), bf16[128,8,2,1024]{3,0,1,2:T(8,128)(2,1)}) %reduce-scatter.2.cloned.1.call-update) | async-done | bytes 4194320 | tf_op jit(solution)/shard_map/reduce_scatter | solution.py:197
  942.4 4.0 fusion.86
  952.7 4.1 copy.43
  957.9 10.9 fusion.25
  972.3 6.2 fusion.46
  978.5 111.4 %all-reduce.3.cloned.1.call-done = (f32[1024,4]{0,1:T(4,128)}, f32[4,1024]{1,0:T(4,128)}, f32[1024,4]{0,1:T(4,128)}, f32[4,1024]{1,0:T(4,128)}) async-done(((f32[1024,4]{0,1:T(4,128)}, f32[4,1024]{1,0:T(4,128)}, f32[1024,4]{0,1:T(4,128)}, f32[4,1024]{1,0:T(4,128)}), (f32[1024,4]{0,1:T(4,128)}, f32[4,1024]{1,0:T(4,128)}, f32[1024,4]{0,1:T(4,128)}, f32[4,1024]{1,0:T(4,128)})) %all-reduce.3.cloned.1.call-update) | async-done | bytes 65552 | tf_op jit(solution)/shard_map/psum | solution.py:220
  (150 shorter events, 57.9 us)
Async XLA Ops:
  7.2 380.1 %copy-start = (bf16[1024,1024]{1,0:T(8,128)(2,1)S(1)}, bf16[1024,1024]{1,0:T(8,128)(2,1)}, u32[]{:S(2)}) copy-start(bf16[1024,1024]{1,0:T(8,128)(2,1)} %param.27) | copy-start | bytes 6291460
  7.2 173.7 %all-gather.5.cloned.1.call-start = ((), (), s32[]{:S(2)}) async-start(), calls=%async_computation.2 | async-start | bytes 18874368 | tf_op jit(solution)/shard_map/all_gather | solution.py:99
  7.2 6.9 copy-start.4
  8.1 5.5 copy-start.24
  8.9 6.1 copy-start.44
  15.0 6.7 copy-start.2
  21.7 5.1 copy-start.13
  21.7 5.2 copy-start.37
  21.7 5.2 copy-start.30
  21.8 8.1 copy-start.28
  26.9 304.9 %all-gather.3.cloned.1.call-start = ((), (), s32[]{:S(2)}) async-start(), calls=%async_computation.1 | async-start | bytes 18874368 | tf_op jit(solution)/shard_map/all_gather | solution.py:100
  29.8 4.6 copy-start.36
  29.9 5.2 copy-start.26
  29.9 8.3 copy-start.34
  34.3 908.1 %reduce-scatter.2.cloned.1.call-start = ((), (), s32[]{:S(2)}) async-start(), calls=%async_computation.3 | async-start | bytes 37748736 | tf_op jit(solution)/shard_map/reduce_scatter | solution.py:197
  49.7 5.8 copy-start.43
  390.1 13.3 %copy-start.9 = (f32[1024,1024]{1,0:T(8,128)}, f32[1024,1024]{1,0:T(8,128)S(1)}, u32[]{:S(2)}) copy-start(f32[1024,1024]{1,0:T(8,128)S(1)} %get-tuple-element.23) | copy-start | bytes 12582916
  390.7 12.7 %copy-start.32 = (f32[4096]{0:T(1024)S(1)}, f32[4096]{0:T(1024)}, u32[]{:S(2)}) copy-start(f32[4096]{0:T(1024)} %convert_element_type.150) | copy-start | bytes 49156
  457.6 34.5 %copy-start.14 = (bf16[8,128,16,64]{1,3,2,0:T(8,128)(2,1)}, bf16[8,128,16,64]{1,3,2,0:T(8,128)(2,1)S(1)}, u32[]{:S(2)}) copy-start(bf16[8,128,16,64]{1,3,2,0:T(8,128)(2,1)S(1)} %copy.36) | copy-start | bytes 6291460
  492.1 43.5 %copy-start.8 = (bf16[8,128,16,64]{1,3,2,0:T(8,128)(2,1)S(1)}, bf16[8,128,16,64]{1,3,2,0:T(8,128)(2,1)}, u32[]{:S(2)}) copy-start(bf16[8,128,16,64]{1,3,2,0:T(8,128)(2,1)} %copy.33) | copy-start | bytes 6291460
  618.5 471.4 %all-reduce.3.cloned.1.call-start = ((), (), s32[]{:S(2)}) async-start(), calls=%async_computation.4 | async-start | bytes 131072 | tf_op jit(solution)/shard_map/psum | solution.py:220
  644.1 5.0 copy-start.10
  644.1 5.0 copy-start.33
  667.1 279.3 %copy-start.29 = (bf16[4,1024]{1,0:T(4,128)(2,1)S(1)}, bf16[4,1024]{1,0:T(4,128)(2,1)}, u32[]{:S(2)}) copy-start(bf16[4,1024]{1,0:T(4,128)(2,1)} %param.38) | copy-start | bytes 24580
  667.1 280.7 %copy-start.16 = (bf16[1024,4]{0,1:T(4,128)(2,1)S(1)}, bf16[1024,4]{0,1:T(4,128)(2,1)}, u32[]{:S(2)}) copy-start(bf16[1024,4]{0,1:T(4,128)(2,1)} %copy-done.15) | copy-start | bytes 24580
  957.9 10.9 copy-start.6
  957.9 10.9 copy-start.12
  957.9 10.9 copy-start.21
  957.9 10.9 copy-start.23
  957.9 10.9 copy-start.25
  957.9 10.9 copy-start.31
  972.3 122.9 %copy-start.1 = (bf16[1024,1024]{1,0:T(8,128)(2,1)S(1)}, bf16[1024,1024]{1,0:T(8,128)(2,1)}, u32[]{:S(2)}) copy-start(bf16[1024,1024]{1,0:T(8,128)(2,1)} %param.27) | copy-start | bytes 6291460
  (19 other events, 52.0 us)
Sparse Core Ops, SparseCore 0:
  27.0 153.7 all-gather.4
  182.4 149.2 all-gather.2
  618.6 323.7 reduce-scatter.1
  972.4 117.4 all-reduce.2
where the time goes:
time: 1110 us; the launch traced here: 1100 us
  waiting for transfers between devices  585 us (53%)
  matrix products  288 us (26%)
  local copies, waits for them, and re-layouts  144 us (13%)
  other arithmetic  70.1 us (6%)
  between operations  14.6 us (1%)
    reduce_scatter x1, waiting for transfers between devices, body(): lax.psum_scatter(stacked.astype(jnp.bfloat16), 'blk', scatter_dimension=0...  275 us
    all_gather x1, waiting for transfers between devices, body(): key_piece = lax.all_gather(key_blocks, 'blk', axis=1, tiled=True)  125 us
    psum x1, waiting for transfers between devices, body(): lax.psum((query_down_grad, query_up_grad, value_down_grad, value_up_grad)...  111 us
    all_gather x1, waiting for transfers between devices, body(): value_piece = lax.all_gather(value_blocks, 'blk', axis=1, tiled=True)  73.4 us
    dot_general x7, matrix products, against(): lax.dot_general(left, right, (((1,), (1,)), ((), ())), preferred_element_...  54.2 us
    dot_general x1, matrix products, body(): jnp.einsum('sqhd,skhd->shqk', d_mixed_heads, value_heads_all, preferred_e...  43.5 us
    another operation x2, local copies, waits for them, and re-layouts, body(): jnp.stack((d_keys_all.reshape(length_all, seqs_here, width), d_values_all...  43.1 us
    dot_general x1, matrix products, body(): jnp.einsum('sqhd,skhd->shqk', query_heads, key_heads, preferred_element_t...  32.1 us
  transfers between devices with their start and end apart: 4, of which 4 were waited for; matrix products, arithmetic and copies ran while one was open for 14% of the time, Pallas kernels for 0%

commit v1 on v0

--- a/solution.py
+++ b/solution.py
@@ -3,10 +3,14 @@
 import jax
 import jax.numpy as jnp
 from jax import lax
+from jax.experimental import pallas as pl
+from jax.experimental.pallas import tpu as pltpu
 from jax.sharding import PartitionSpec as P
 
 HD = 64
 RANK = 4
+LANES = 128
+STEP = 256
 
 
 epsilon = 1e-05
@@ -36,6 +40,243 @@
     return lax.dot_general(
         left, right, (((1,), (1,)), ((), ())), preferred_element_type=jnp.float32
     )
+
+def nt(a, b):
+    return lax.dot_general(a, b, (((1,), (1,)), ((), ())), preferred_element_type=jnp.float32)
+
+def tn(a, b):
+    return lax.dot_general(a, b, (((0,), (0,)), ((), ())), preferred_element_type=jnp.float32)
+
+def thirds(x):
+    first = x.astype(jnp.bfloat16)
+    rest = x - first.astype(jnp.float32)
+    second = rest.astype(jnp.bfloat16)
+    third = (rest - second.astype(jnp.float32)).astype(jnp.bfloat16)
+    return first, second, third
+
+def lanes_of(head):
+    lane = lax.broadcasted_iota(jnp.int32, (1, LANES), 1)
+    own = (lane // HD) == head
+    spare = lane - HD * (1 - head)
+    return own, spare
+
+def at_spare(spare, start, parts, rest):
+    for index, part in enumerate(parts):
+        rest = jnp.where(spare == start + index, part, rest)
+    return rest
+
+def forward_kernel(lengths, q_ref, k_ref, v_ref, mixed_ref, aux_ref):
+    length = lengths[pl.program_id(0)]
+    rows = q_ref.shape[0]
+    zero, one = jnp.bfloat16(0), jnp.bfloat16(1)
+    place = lax.broadcasted_iota(jnp.int32, (rows, LANES), 0)
+    bias = jnp.where(place < length, jnp.float32(0), jnp.float32(masked_value)).astype(jnp.bfloat16)
+    causal = lax.broadcasted_iota(jnp.int32, (STEP, STEP), 1) <= lax.broadcasted_iota(jnp.int32, (STEP, STEP), 0)
+    q, k, v = q_ref[...] * jnp.bfloat16(HD ** -0.5), k_ref[...], v_ref[...]
+    own = [lanes_of(h)[0] for h in range(2)]
+    spare = [lanes_of(h)[1] for h in range(2)]
+    k_aug = [jnp.where(own[h], k, jnp.where(spare[h] == 0, bias, jnp.where((spare[h] > 0) & (spare[h] < 4), one, zero))) for h in range(2)]
+    q_aug = [jnp.where(own[h], q, jnp.where(spare[h] == 0, one, zero)) for h in range(2)]
+    for start in range(0, rows, STEP):
+        stop = start + STEP
+        outs, auxs = [], []
+        for h in range(2):
+            s = nt(q_aug[h][start:stop], k_aug[h][:stop])
+            edge = jnp.where(causal, s[:, start:stop], masked_value)
+            s = edge if start == 0 else jnp.concatenate([s[:, :start], edge], axis=1)
+            top = jnp.max(s, axis=1, keepdims=True)
+            w = jnp.exp(s - top)
+            total = jnp.sum(w, axis=1, keepdims=True)
+            o = jnp.dot(w.astype(jnp.bfloat16), v[:stop], preferred_element_type=jnp.float32)
+            outs.append(o / total)
+            parts = thirds(-(top + jnp.log(total)))
+            auxs.append(at_spare(spare[h], 1, parts, jnp.where(spare[h] == 0, one, zero)))
+        mixed_ref[start:stop] = jnp.where(own[0], outs[0], outs[1]).astype(jnp.bfloat16)
+        aux_ref[start:stop] = jnp.where(own[0], auxs[1], auxs[0])
+
+def backward_kernel(lengths, q_ref, k_ref, v_ref, mixed_ref, aux_ref, do_ref, dq_ref, dk_ref, dv_ref, acc):
+    length = lengths[pl.program_id(0)]
+    rows = q_ref.shape[0]
+    zero, one = jnp.bfloat16(0), jnp.bfloat16(1)
+    place = lax.broadcasted_iota(jnp.int32, (rows, LANES), 0)
+    bias = jnp.where(place < length, jnp.float32(0), jnp.float32(masked_value)).astype(jnp.bfloat16)
+    causal = lax.broadcasted_iota(jnp.int32, (STEP, STEP), 0) <= lax.broadcasted_iota(jnp.int32, (STEP, STEP), 1)
+    q, k, v, do, aux = q_ref[...] * jnp.bfloat16(HD ** -0.5), k_ref[...], v_ref[...], do_ref[...], aux_ref[...]
+    product = do.astype(jnp.float32) * mixed_ref[...].astype(jnp.float32)
+    own = [lanes_of(h)[0] for h in range(2)]
+    spare = [lanes_of(h)[1] for h in range(2)]
+    k_aug = [jnp.where(own[h], k, jnp.where(spare[h] == 0, bias, jnp.where((spare[h] > 0) & (spare[h] < 4), one, zero))) for h in range(2)]
+    q_aug = [jnp.where(own[h], q, aux) for h in range(2)]
+    v_aug = [jnp.where(own[h], v, jnp.where((spare[h] >= 0) & (spare[h] < 3), one, zero)) for h in range(2)]
+    do_aug = []
+    for h in range(2):
+        delta = jnp.sum(jnp.where(own[h], product, 0.0), axis=1, keepdims=True)
+        do_aug.append(jnp.where(own[h], do, at_spare(spare[h], 0, thirds(-delta), zero)))
+    for start in range(0, rows, STEP):
+        stop = start + STEP
+        dks, dvs, dqs = [], [], []
+        for h in range(2):
+            s = nt(k_aug[h][start:stop], q_aug[h][start:])
+            edge = jnp.where(causal, s[:, :STEP], masked_value)
+            s = edge if stop == rows else jnp.concatenate([edge, s[:, STEP:]], axis=1)
+            p = jnp.exp(s)
+            dp = nt(v_aug[h][start:stop], do_aug[h][start:])
+            ds = (p * dp).astype(jnp.bfloat16)
+            dvs.append(jnp.dot(p.astype(jnp.bfloat16), do[start:], preferred_element_type=jnp.float32))
+            dks.append(jnp.dot(ds, q[start:], preferred_element_type=jnp.float32))
+            dqs.append(tn(ds, k[start:stop]))
+        dv_ref[start:stop] = jnp.where(own[0], dvs[0], dvs[1]).astype(jnp.bfloat16)
+        dk_ref[start:stop] = jnp.where(own[0], dks[0], dks[1]).astype(jnp.bfloat16)
+        dq = jnp.where(own[0], dqs[0], dqs[1])
+        if start == 0:
+            acc[...] = dq
+        else:
+            acc[start:] += dq
+    dq_ref[...] = (acc[...] * HD ** -0.5).astype(jnp.bfloat16)
+
+def column(offset):
+    return lambda slot, pair, lengths: (slot, offset + pair)
+
+def attention_forward(lengths, qkv, width):
+    slots = lengths.shape[0]
+    rows = qkv.shape[0] // slots
+    pairs = width // LANES
+    spec = lambda offset: pl.BlockSpec((rows, LANES), column(offset))
+    return pl.pallas_call(
+        forward_kernel,
+        grid_spec=pltpu.PrefetchScalarGridSpec(
+            num_scalar_prefetch=1, grid=(slots, pairs),
+            in_specs=[spec(0), spec(pairs), spec(2 * pairs)],
+            out_specs=[spec(0), spec(0)]),
+        out_shape=[jax.ShapeDtypeStruct((slots * rows, width), jnp.bfloat16)] * 2,
+        compiler_params=pltpu.CompilerParams(vmem_limit_bytes=48 << 20),
+        name="attention_forward",
+    )(lengths, qkv, qkv, qkv)
+
+def attention_backward(lengths, qkv, mixed, aux, d_mixed, width):
+    slots = lengths.shape[0]
+    rows = qkv.shape[0] // slots
+    pairs = width // LANES
+    spec = lambda offset: pl.BlockSpec((rows, LANES), column(offset))
+    return pl.pallas_call(
+        backward_kernel,
+        grid_spec=pltpu.PrefetchScalarGridSpec(
+            num_scalar_prefetch=1, grid=(slots, pairs),
+            in_specs=[spec(0), spec(pairs), spec(2 * pairs), spec(0), spec(0), spec(0)],
+            out_specs=[spec(0)] * 3,
+            scratch_shapes=[pltpu.VMEM((rows, LANES), jnp.float32)]),
+        out_shape=[jax.ShapeDtypeStruct((slots * rows, width), jnp.bfloat16)] * 3,
+        compiler_params=pltpu.CompilerParams(vmem_limit_bytes=48 << 20),
+        name="attention_backward",
+    )(lengths, qkv, qkv, qkv, mixed, aux, d_mixed)
+
+
+def whole_slots(
+    tokens,
+    lengths,
+    norm_gain,
+    norm_shift,
+    joint_weight,
+    query_bias,
+    value_bias,
+    output_weight,
+    output_bias,
+    second_gain,
+    second_shift,
+    upward_weight,
+    upward_bias,
+    down_weight,
+    down_bias,
+    query_down,
+    query_up,
+    value_down,
+    value_up,
+    cotangent,
+):
+    seqs_here, rows, width = tokens.shape
+    ranks = lax.axis_size("blk")
+    slots = seqs_here // ranks
+    adapter = 32.0 / RANK
+    positions = slots * rows * ranks
+
+    def to_slots(v):
+        pieces = lax.all_to_all(
+            v.reshape(ranks, slots, rows, width), "blk", 0, 0, tiled=True
+        )
+        return jnp.swapaxes(pieces, 0, 1).reshape(positions, width)
+
+    def to_rows(v):
+        pieces = jnp.swapaxes(v.reshape(slots, ranks, rows, width), 0, 1)
+        return lax.all_to_all(pieces, "blk", 0, 0, tiled=True).reshape(seqs_here, rows, width)
+
+    my_lengths = lax.dynamic_slice_in_dim(lengths, lax.axis_index("blk") * slots, slots)
+    flat = to_slots(tokens).astype(jnp.float32)
+    outer = to_slots(cotangent)
+    normed_full, standard, inverse = normalize(flat, norm_gain, norm_shift)
+    normed = normed_full.astype(jnp.bfloat16)
+    joint = jnp.dot(normed, joint_weight, preferred_element_type=jnp.float32)
+    query_low = jnp.dot(normed, query_down, preferred_element_type=jnp.float32).astype(jnp.bfloat16)
+    value_low = jnp.dot(normed, value_down, preferred_element_type=jnp.float32).astype(jnp.bfloat16)
+    bias = jnp.concatenate((query_bias, jnp.zeros_like(query_bias), value_bias)).astype(jnp.float32)
+    lows = jnp.concatenate((query_low, value_low), axis=1)
+    nothing = jnp.zeros_like(query_up)
+    ups = jnp.concatenate(
+        (
+            jnp.concatenate((query_up, nothing, nothing), axis=1),
+            jnp.concatenate((nothing, nothing, value_up), axis=1),
+        ),
+        axis=0,
+    )
+    qkv = (
+        joint + bias + adapter * jnp.dot(lows, ups, preferred_element_type=jnp.float32)
+    ).astype(jnp.bfloat16)
+    mixed, aux = attention_forward(my_lengths, qkv, width)
+    middle = (
+        flat
+        + jnp.dot(mixed, output_weight, preferred_element_type=jnp.float32)
+        + output_bias.astype(jnp.float32)
+    )
+    normed_two_full, standard_two, inverse_two = normalize(middle, second_gain, second_shift)
+    normed_two = normed_two_full.astype(jnp.bfloat16)
+    hidden = jnp.dot(
+        normed_two, upward_weight, preferred_element_type=jnp.float32
+    ) + upward_bias.astype(jnp.float32)
+    active_full, gelu_pull = jax.vjp(partial(jax.nn.gelu, approximate=True), hidden)
+    active = active_full.astype(jnp.bfloat16)
+    block_output = (
+        middle
+        + jnp.dot(active, down_weight, preferred_element_type=jnp.float32)
+        + down_bias.astype(jnp.float32)
+    ).astype(jnp.bfloat16)
+    block_output = to_rows(block_output)
+    d_active = against(outer, down_weight)
+    d_hidden = gelu_pull(d_active)[0].astype(jnp.bfloat16)
+    d_normed_two = against(d_hidden, upward_weight)
+    d_middle = outer.astype(jnp.float32) + norm_back(
+        d_normed_two, standard_two, inverse_two, second_gain
+    )
+    d_mixed = against(d_middle.astype(jnp.bfloat16), output_weight).astype(jnp.bfloat16)
+    d_query_low, d_key_low, d_value_low = attention_backward(
+        my_lengths, qkv, mixed, aux, d_mixed, width
+    )
+    query_up_grad = adapter * transposed(query_low, d_query_low)
+    value_up_grad = adapter * transposed(value_low, d_value_low)
+    d_query_small = (adapter * against(d_query_low, query_up)).astype(jnp.bfloat16)
+    d_value_small = (adapter * against(d_value_low, value_up)).astype(jnp.bfloat16)
+    query_down_grad = transposed(normed, d_query_small)
+    value_down_grad = transposed(normed, d_value_small)
+    d_joint = jnp.concatenate((d_query_low, d_key_low, d_value_low), axis=1)
+    d_normed = (
+        against(d_joint, joint_weight)
+        + against(d_query_small, query_down)
+        + against(d_value_small, value_down)
+    )
+    token_grads = d_middle + norm_back(d_normed, standard, inverse, norm_gain)
+    token_grads = to_rows(token_grads.astype(jnp.bfloat16)).astype(jnp.float32)
+    sums = lax.psum(
+        (query_down_grad, query_up_grad, value_down_grad, value_up_grad), ("batch", "blk")
+    )
+    return (block_output, token_grads, sums[0], sums[1], sums[2], sums[3])
 
 
 def body(
@@ -223,6 +464,11 @@
     return (block_output, token_grads, sums[0], sums[1], sums[2], sums[3])
 
 
+def choose(tokens, *others):
+    fits = tokens.shape[0] % lax.axis_size("blk") == 0
+    return (whole_slots if fits else body)(tokens, *others)
+
+
 def solution(mesh):
     placed = (
         P("batch", "blk", None),
@@ -247,7 +493,7 @@
         P("batch", "blk", None),
     )
     return jax.shard_map(
-        body,
+        choose,
         mesh=mesh,
         in_specs=placed,
         out_specs=(P("batch", "blk", None), P("batch", "blk", None), P(), P(), P(), P()),

time: 1110 us -> 460 us (0.41)
  waiting for transfers between devices: 585 us -> 206 us
  matrix products: 288 us -> 111 us
  local copies, waits for them, and re-layouts: 144 us -> 9.27 us
  Pallas kernels: 0 us -> 68.4 us
  other arithmetic: 70.1 us -> 20 us
  starting transfers between devices: 0.16 us -> 20.6 us
    reduce_scatter x1 -> x0, waiting for transfers between devices: 275 us -> none  [body(): lax.psum_scatter(stacked.astype(jnp.bfloat16), 'blk', scatter_dimension=0...]
    all_gather x2 -> x0, waiting for transfers between devices: 198 us -> none  [the longest x1 125 us: body(): key_piece = lax.all_gather(key_blocks, 'blk', axis=1, tiled=True)]
    dot_general x14 -> x7, matrix products: 230 us -> 48.7 us  [the longest x1 18.3 us: whole_slots(): jnp.dot(active, down_weight, preferred_element_type=jnp.float32)]
    all_to_all x0 -> x4, waiting for transfers between devices: none -> 117 us  [the longest x2 69.1 us: to_rows(): lax.all_to_all(pieces, 'blk', 0, 0, tiled=True)]
    pallas_call x0 -> x2, Pallas kernels: none -> 68.4 us  [the longest x1 36.9 us: attention_backward(): pl.pallas_call(backward_kernel, grid_spec=pltpu.PrefetchScalarGridSpec(nu...]
    all_gather x2 -> x0, local copies, waits for them, and re-layouts: 43.8 us -> none  [the longest x1 22.3 us: body(): key_piece = lax.all_gather(key_blocks, 'blk', axis=1, tiled=True)]
    another operation x2 -> x0, local copies, waits for them, and re-layouts: 43.1 us -> none  [body(): jnp.stack((d_keys_all.reshape(length_all, seqs_here, width), d_values_all...]
    reduce_sum x2 -> x0, other arithmetic: 26.4 us -> none  [the longest x1 22.5 us: body(): totals = jnp.sum(weights, axis=-1)]
  transfers between devices with their start and end apart: 4 -> 5, of which waited for: 4 -> 4; matrix products, arithmetic and copies ran while one was open for 14% -> 15% of each run, Pallas kernels for 0% -> 7%
where the time goes in v1:
time: 460 us; the launch traced here: 450 us
  waiting for transfers between devices  206 us (45%)
  matrix products  111 us (24%)
  Pallas kernels  68.4 us (15%)
  starting transfers between devices  20.6 us (4%)
  other arithmetic  20 us (4%)
  between operations  14.9 us (3%)
  local copies, waits for them, and re-layouts  9.27 us (2%)
    psum x1, waiting for transfers between devices, whole_slots(): lax.psum((query_down_grad, query_up_grad, value_down_grad, value_up_grad)...  88.7 us
    all_to_all x2, waiting for transfers between devices, to_rows(): lax.all_to_all(pieces, 'blk', 0, 0, tiled=True)  69.1 us
    dot_general x7, matrix products, against(): lax.dot_general(left, right, (((1,), (1,)), ((), ())), preferred_element_...  55.1 us
    all_to_all x2, waiting for transfers between devices, to_slots(): lax.all_to_all(v.reshape(ranks, slots, rows, width), 'blk', 0, 0, tiled=T...  48.3 us
    pallas_call x1, Pallas kernels, attention_backward(): pl.pallas_call(backward_kernel, grid_spec=pltpu.PrefetchScalarGridSpec(nu...  36.9 us
    pallas_call x1, Pallas kernels, attention_forward(): pl.pallas_call(forward_kernel, grid_spec=pltpu.PrefetchScalarGridSpec(num...  31.5 us
    dot_general x1, matrix products, whole_slots(): jnp.dot(active, down_weight, preferred_element_type=jnp.float32)  18.3 us
    dot_general x1, matrix products, whole_slots(): jnp.dot(normed_two, upward_weight, preferred_element_type=jnp.float32)  12.3 us
  transfers between devices with their start and end apart: 5, of which 4 were waited for; matrix products, arithmetic and copies ran while one was open for 15% of the time, Pallas kernels for 7%

profile of v1, /device:TPU:0, one launch (start us, length us, event | category | flops | bytes accessed | tf_op | source)
XLA Modules:
  0.0 450.4 jit_solution(696876983839686489)
XLA Ops:
  7.3 6.5 %all-to-all-start = ((bf16[8,1,128,1024]{3,2,1,0:T(8,128)(2,1)}), bf16[8,1,128,1024]{3,2,1,0:T(8,128)(2,1)}, u32[]{:S(2)}, u32[]{:S(2)}) async-start(bf16[8,1,128,1024]{3,2,1,0:T(8,128)(2,1)} %bitcast.77), calls=%async_computation | async-start | bytes 4194304 | tf_op jit(solution)/shard_map/all_to_all | solution.py:203
  14.6 48.3 %all-to-all-done = bf16[8,1,128,1024]{3,2,1,0:T(8,128)(2,1)} async-done(((bf16[8,1,128,1024]{3,2,1,0:T(8,128)(2,1)}), bf16[8,1,128,1024]{3,2,1,0:T(8,128)(2,1)}, u32[]{:S(2)}, u32[]{:S(2)}) %all-to-all-start) | async-done | bytes 2097184 | tf_op jit(solution)/shard_map/all_to_all | solution.py:203
  62.9 4.4 all-to-all-start.2
  67.3 2.1 convert_reduce_fusion
  69.4 2.3 fusion.17
  71.8 2.6 fusion.23
  75.8 6.7 %fusion.73 = f32[1024,3072]{1,0:T(8,128)S(1)} fusion(bf16[1024,1024]{1,0:T(8,128)(2,1)S(1)} %fusion.23, bf16[1024,3072]{1,0:T(8,128)(2,1)S(1)} %bitcast.83), kind=kOutput, calls=%fused_computation.101 | convolution fusion | flops 6442450944 | bytes 20971520 | tf_op jit(solution)/shard_map/dot_general | solution.py:217
  82.5 4.5 %add_convert_fusion.q_ref.k_ref.v_ref = bf16[1024,3072]{1,0:T(8,128)(2,1)} fusion(f32[1024,3072]{1,0:T(8,128)S(1)} %fusion.73, f32[3072]{0:T(1024)S(1)} %maximum_convert_fusion, bf16[4,1024]{1,0:T(4,128)(2,1)S(1)} %copy-done.20, bf16[4,1024]{1,0:T(4,128)(2,1)S(1)} %copy-done.19, bf16[1024,4]{0,1:T(4,128)(2,1)S(1)} %convolution_convert_fusion, ...), kind=kOutput, calls=%fused_computation.10 | convolution fusion | flops 63143936 | bytes 18919424 | tf_op jit(solution)/shard_map/dot_general | solution.py:231
  87.0 31.5 %attention_forward.1 = (bf16[1024,1024]{1,0:T(8,128)(2,1)S(1)}, bf16[1024,1024]{1,0:T(8,128)(2,1)S(1)}) custom-call(s32[1]{0:T(128)} %dynamic_slice.3.lengths, bf16[1024,3072]{1,0:T(8,128)(2,1)} %add_convert_fusion.q_ref.k_ref.v_ref, bf16[1024,3072]{1,0:T(8,128)(2,1)} %add_convert_fusion.q_ref.k_ref.v_ref, bf16[1024,3072]{1,0:T(8,128)(2,1)} %add_convert_fusion.q_ref.k_ref.v_ref), custom_call_target="tpu_custom_call" | custom-call | tf_op jit(solution)/shard_map/attention_forward/pallas_call | solution.py:145
  118.6 5.6 %fusion.70 = (f32[1024]{0:T(1024)S(1)}, f32[1024,1024]{1,0:T(8,128)S(1)}) fusion(f32[1024]{0:T(1024)S(1)} %convert_element_type.98, bf16[1024,1024]{1,0:T(8,128)(2,1)S(1)} %get-tuple-element.11.mixed_ref, bf16[1024,1024]{1,0:T(8,128)(2,1)S(1)} %copy-done, bf16[8,1,128,1024]{3,2,1,0:T(8,128)(2,1)} %all-to-all-done), kind=kOutput, calls=%fused_computation.99 | convolution fusion | flops 2151676928 | bytes 10493952 | tf_op jit(solution)/shard_map/dot_general | solution.py:236
  124.8 1.4 copy-done.6
  126.2 12.3 %fusion.30 = f32[1024,4096]{1,0:T(8,128)} fusion(bf16[1024,4096]{1,0:T(8,128)(2,1)S(1)} %bitcast.81, f32[1024,1024]{1,0:T(8,128)S(1)} %get-tuple-element.27, f32[1024]{0:T(1024)S(1)} %convert_element_type.100, f32[1024]{0:T(1024)S(1)} %convert_element_type.99, f32[1024]{0:T(1024)S(1)} %add_rsqrt_fusion, f32[1024]{0:T(1024)S(1)} %broadcast_multiply_fusion.4), kind=kOutput, calls=%fused_computation.45 | convolution fusion | flops 8595177472 | bytes 29376512 | tf_op jit(solution)/shard_map/dot_general | solution.py:241
  138.5 32.7 %multiply_reduce_fusion.2 = (f32[1024]{0:T(1024)S(1)}, f32[1024]{0:T(1024)S(1)}, f32[1024,1024]{1,0:T(8,128)}) fusion(f32[1024]{0:T(1024)S(1)} %convert_element_type.99, f32[1024]{0:T(1024)S(1)} %add_rsqrt_fusion, f32[1024,1024]{1,0:T(8,128)} %copy-done.6, f32[1024]{0:T(1024)S(1)} %broadcast_multiply_fusion.4, bf16[1024,4096]{1,0:T(8,128)(2,1)} %param.31, ...), kind=kOutput, calls=%fused_computation.44 | convolution fusion | flops 17274241024 | bytes 44077056 | tf_op jit(solution)/shard_map/dot_general | solution.py:40
  171.2 4.7 %multiply_add_fusion = f32[1024,1024]{1,0:T(8,128)S(1)} fusion(f32[1024,1024]{1,0:T(8,128)} %get-tuple-element.28, f32[1024,1024]{1,0:T(8,128)} %copy-done.6, f32[1024]{0:T(1024)S(1)} %get-tuple-element.30, f32[1024]{0:T(1024)S(1)} %get-tuple-element.31, f32[1024]{0:T(1024)S(1)} %convert_element_type.99, f32[1024]{0:T(1024)S(1)} %add_rsqrt_fusion, ...), kind=kLoop, calls=%fused_computation.38 | loop fusion | flops 9437184 | bytes 14700544 | tf_op jit(solution)/shard_map/add | solution.py:255
  176.0 3.7 fusion.37.do_ref
  179.7 36.9 %attention_backward.1 = (bf16[1024,1024]{1,0:T(8,128)(2,1)S(1)}, bf16[1024,1024]{1,0:T(8,128)(2,1)S(1)}, bf16[1024,1024]{1,0:T(8,128)(2,1)}) custom-call(s32[1]{0:T(128)} %dynamic_slice.3.lengths, bf16[1024,3072]{1,0:T(8,128)(2,1)} %add_convert_fusion.q_ref.k_ref.v_ref, bf16[1024,3072]{1,0:T(8,128)(2,1)} %add_convert_fusion.q_ref.k_ref.v_ref, ...), custom_call_target="tpu_custom_call" | custom-call | tf_op jit(solution)/shard_map/attention_backward/pallas_call | solution.py:161
  217.3 3.0 fusion.41
  220.3 11.0 %fusion.10 = f32[1024,1024]{1,0:T(8,128)} fusion(bf16[1024,3072]{1,0:T(8,128)(2,1)} %param.24, bf16[1024,1024]{1,0:T(8,128)(2,1)S(1)} %copy-done.7, bf16[1024,1024]{1,0:T(8,128)(2,1)S(1)} %get-tuple-element.14, bf16[1024,1024]{1,0:T(8,128)(2,1)S(1)} %get-tuple-element.13), kind=kOutput, calls=%fused_computation.13 | convolution fusion | flops 6461325312 | bytes 16777216 | tf_op jit(solution)/shard_map/dot_general | solution.py:40
  232.1 1.4 copy-done.8
  233.5 3.3 fusion.69
  236.8 3.7 fusion.28
  240.5 5.4 %all-to-all-start.3 = ((bf16[8,1,128,1024]{3,2,1,0:T(8,128)(2,1)}), bf16[8,1,128,1024]{3,2,1,0:T(8,128)(2,1)}, u32[]{:S(2)}, u32[]{:S(2)}) async-start(bf16[8,1,128,1024]{3,2,1,0:T(8,128)(2,1)} %bitcast.76), calls=%async_computation.3 | async-start | bytes 4194304 | tf_op jit(solution)/shard_map/all_to_all | solution.py:210
  245.9 18.3 %add_convert_fusion.1 = bf16[1024,1024]{1,0:T(8,128)(2,1)} fusion(f32[1024,1024]{1,0:T(8,128)} %copy-done.6, f32[1024]{0:T(1024)S(1)} %convert_element_type.104, bf16[4096,1024]{1,0:T(8,128)(2,1)} %param.33, f32[1024,4096]{1,0:T(8,128)} %fusion.30, f32[4096]{0:T(1024)S(1)} %convert_element_type.102), kind=kOutput, calls=%fused_computation.40 | convolution fusion | flops 8635023360 | bytes 31477760 | tf_op jit(solution)/shard_map/dot_general | solution.py:248
  264.2 30.8 %all-to-all-done.3 = bf16[8,1,128,1024]{3,2,1,0:T(8,128)(2,1)} async-done(((bf16[8,1,128,1024]{3,2,1,0:T(8,128)(2,1)}), bf16[8,1,128,1024]{3,2,1,0:T(8,128)(2,1)}, u32[]{:S(2)}, u32[]{:S(2)}) %all-to-all-start.3) | async-done | bytes 2097184 | tf_op jit(solution)/shard_map/all_to_all | solution.py:210
  295.0 4.4 all-to-all-start.1
  299.4 2.7 convolution_multiply_fusion.1
  302.1 2.6 convolution_multiply_fusion
  305.7 1.0 fusion.75
  306.7 4.1 bitcast_convert_fusion
  310.8 38.3 %all-to-all-done.1 = bf16[8,1,128,1024]{3,2,1,0:T(8,128)(2,1)} async-done(((bf16[8,1,128,1024]{3,2,1,0:T(8,128)(2,1)}), bf16[8,1,128,1024]{3,2,1,0:T(8,128)(2,1)}, u32[]{:S(2)}, u32[]{:S(2)}) %all-to-all-start.1) | async-done | bytes 2097184 | tf_op jit(solution)/shard_map/all_to_all | solution.py:210
  349.1 88.7 %all-reduce.5.cloned.1.call-done = (f32[1024,4]{0,1:T(4,128)}, f32[4,1024]{1,0:T(4,128)}, f32[1024,4]{0,1:T(4,128)}, f32[4,1024]{1,0:T(4,128)}) async-done(((f32[1024,4]{0,1:T(4,128)}, f32[4,1024]{1,0:T(4,128)}, f32[1024,4]{0,1:T(4,128)}, f32[4,1024]{1,0:T(4,128)}), (f32[1024,4]{0,1:T(4,128)}, f32[4,1024]{1,0:T(4,128)}, f32[1024,4]{0,1:T(4,128)}, f32[4,1024]{1,0:T(4,128)})) %all-reduce.5.cloned.1.call-update) | async-done | bytes 65552 | tf_op jit(solution)/shard_map/psum | solution.py:276
  437.8 3.1 copy.33
  (116 shorter events, 7.7 us)
Async XLA Ops:
  7.2 111.4 %copy-start = (bf16[1024,1024]{1,0:T(8,128)(2,1)S(1)}, bf16[1024,1024]{1,0:T(8,128)(2,1)}, u32[]{:S(2)}) copy-start(bf16[1024,1024]{1,0:T(8,128)(2,1)} %param.27) | copy-start | bytes 6291460
  7.2 6.6 %copy-start.30 = (bf16[1024]{0:T(1024)(128)(2,1)S(1)}, bf16[1024]{0:T(1024)(128)(2,1)}, u32[]{:S(2)}) copy-start(bf16[1024]{0:T(1024)(128)(2,1)} %param.29) | copy-start | bytes 6148
  7.2 6.6 %copy-start.31 = (bf16[1024]{0:T(1024)(128)(2,1)S(1)}, bf16[1024]{0:T(1024)(128)(2,1)}, u32[]{:S(2)}) copy-start(bf16[1024]{0:T(1024)(128)(2,1)} %param.22) | copy-start | bytes 6148
  7.2 6.6 %copy-start.32 = (bf16[1024]{0:T(1024)(128)(2,1)S(1)}, bf16[1024]{0:T(1024)(128)(2,1)}, u32[]{:S(2)}) copy-start(bf16[1024]{0:T(1024)(128)(2,1)} %param.23) | copy-start | bytes 6148
  7.2 6.6 %copy-start.33 = (bf16[1024]{0:T(1024)(128)(2,1)S(1)}, bf16[1024]{0:T(1024)(128)(2,1)}, u32[]{:S(2)}) copy-start(bf16[1024]{0:T(1024)(128)(2,1)} %param.28) | copy-start | bytes 6148
  7.2 6.6 %copy-start.34 = (bf16[1024]{0:T(1024)(128)(2,1)S(1)}, bf16[1024]{0:T(1024)(128)(2,1)}, u32[]{:S(2)}) copy-start(bf16[1024]{0:T(1024)(128)(2,1)} %param.30) | copy-start | bytes 6148
  7.2 6.6 %copy-start.29 = (bf16[4096]{0:T(1024)(128)(2,1)S(1)}, bf16[4096]{0:T(1024)(128)(2,1)}, u32[]{:S(2)}) copy-start(bf16[4096]{0:T(1024)(128)(2,1)} %param.32) | copy-start | bytes 24580
  7.2 6.6 %copy-start.38 = (s32[8]{0:T(128)S(1)}, s32[8]{0:T(128)}, u32[]{:S(2)}) copy-start(s32[8]{0:T(128)} %param.21) | copy-start | bytes 100
  7.3 7.3 %copy-start.35 = (bf16[1024]{0:T(1024)(128)(2,1)S(1)}, bf16[1024]{0:T(1024)(128)(2,1)}, u32[]{:S(2)}) copy-start(bf16[1024]{0:T(1024)(128)(2,1)} %param.26) | copy-start | bytes 6148
  7.3 7.3 %copy-start.36 = (bf16[1024]{0:T(1024)(128)(2,1)S(1)}, bf16[1024]{0:T(1024)(128)(2,1)}, u32[]{:S(2)}) copy-start(bf16[1024]{0:T(1024)(128)(2,1)} %param.25) | copy-start | bytes 6148
  7.3 55.6 %all-to-all-start = ((bf16[8,1,128,1024]{3,2,1,0:T(8,128)(2,1)}), bf16[8,1,128,1024]{3,2,1,0:T(8,128)(2,1)}, u32[]{:S(2)}, u32[]{:S(2)}) async-start(bf16[8,1,128,1024]{3,2,1,0:T(8,128)(2,1)} %bitcast.77), calls=%async_computation | async-start | bytes 4194304 | tf_op jit(solution)/shard_map/all_to_all | solution.py:203
  13.8 57.9 %copy-start.17 = (f32[1024]{0:T(1024)}, f32[1024]{0:T(1024)S(1)}, u32[]{:S(2)}) copy-start(f32[1024]{0:T(1024)S(1)} %convert_element_type.91) | copy-start | bytes 12292
  62.9 75.6 %all-to-all-start.2 = ((bf16[8,1,128,1024]{3,2,1,0:T(8,128)(2,1)}), bf16[8,1,128,1024]{3,2,1,0:T(8,128)(2,1)}, u32[]{:S(2)}, u32[]{:S(2)}) async-start(bf16[8,1,128,1024]{3,2,1,0:T(8,128)(2,1)} %bitcast.78), calls=%async_computation.2 | async-start | bytes 4194304 | tf_op jit(solution)/shard_map/all_to_all | solution.py:203
  67.3 7.0 %copy-start.23 = (bf16[1024,4]{0,1:T(4,128)(2,1)S(1)}, bf16[1024,4]{0,1:T(4,128)(2,1)}, u32[]{:S(2)}) copy-start(bf16[1024,4]{0,1:T(4,128)(2,1)} %param.37) | copy-start | bytes 24580
  67.3 8.4 %slice-start.2 = ((s8[6291456]{0:T(1024)(128)(4,1)}), s8[4194304]{0:T(1024)(128)(4,1)S(1)}, s32[]{:S(2)}) async-start(s8[6291456]{0:T(1024)(128)(4,1)} %bitcast.82), calls=%async_computation.7 | async-start | bytes 8388608
  69.4 5.6 %copy-start.21 = (bf16[1024,4]{0,1:T(4,128)(2,1)S(1)}, bf16[1024,4]{0,1:T(4,128)(2,1)}, u32[]{:S(2)}) copy-start(bf16[1024,4]{0,1:T(4,128)(2,1)} %param.35) | copy-start | bytes 24580
  75.0 7.4 %copy-start.9 = (bf16[1024,4]{0,1:T(4,128)(2,1)}, bf16[1024,4]{0,1:T(4,128)(2,1)S(1)}, u32[]{:S(2)}) copy-start(bf16[1024,4]{0,1:T(4,128)(2,1)S(1)} %convolution_convert_fusion) | copy-start | bytes 24580
  75.7 6.7 %copy-start.11 = (bf16[1024,4]{0,1:T(4,128)(2,1)}, bf16[1024,4]{0,1:T(4,128)(2,1)S(1)}, u32[]{:S(2)}) copy-start(bf16[1024,4]{0,1:T(4,128)(2,1)S(1)} %convolution_convert_fusion.1) | copy-start | bytes 24580
  75.7 6.7 %copy-start.19 = (bf16[4,1024]{1,0:T(4,128)(2,1)S(1)}, bf16[4,1024]{1,0:T(4,128)(2,1)}, u32[]{:S(2)}) copy-start(bf16[4,1024]{1,0:T(4,128)(2,1)} %param.36) | copy-start | bytes 24580
  75.7 6.7 %copy-start.20 = (bf16[4,1024]{1,0:T(4,128)(2,1)S(1)}, bf16[4,1024]{1,0:T(4,128)(2,1)}, u32[]{:S(2)}) copy-start(bf16[4,1024]{1,0:T(4,128)(2,1)} %param.38) | copy-start | bytes 24580
  118.5 5.6 %copy-start.2 = (bf16[1024,1024]{1,0:T(8,128)(2,1)}, bf16[1024,1024]{1,0:T(8,128)(2,1)S(1)}, u32[]{:S(2)}) copy-start(bf16[1024,1024]{1,0:T(8,128)(2,1)S(1)} %get-tuple-element.11.mixed_ref) | copy-start | bytes 6291460
  118.6 5.6 %copy-start.3 = (bf16[1024,1024]{1,0:T(8,128)(2,1)}, bf16[1024,1024]{1,0:T(8,128)(2,1)S(1)}, u32[]{:S(2)}) copy-start(bf16[1024,1024]{1,0:T(8,128)(2,1)S(1)} %get-tuple-element.12.aux_ref) | copy-start | bytes 6291460
  118.6 7.7 %slice-start = ((s8[8388608]{0:T(1024)(128)(4,1)}), s8[4194304]{0:T(1024)(128)(4,1)S(1)}, s32[]{:S(2)}) async-start(s8[8388608]{0:T(1024)(128)(4,1)} %bitcast.80), calls=%async_computation.5 | async-start | bytes 8388608
  118.6 7.6 %slice-start.1 = ((s8[8388608]{0:T(1024)(128)(4,1)}), s8[4194304]{0:T(1024)(128)(4,1)S(1)}, s32[]{:S(2)}) async-start(s8[8388608]{0:T(1024)(128)(4,1)} %bitcast.80), calls=%async_computation.6 | async-start | bytes 8388608
  216.6 14.7 %copy-start.1 = (bf16[1024,1024]{1,0:T(8,128)(2,1)}, bf16[1024,1024]{1,0:T(8,128)(2,1)S(1)}, u32[]{:S(2)}) copy-start(bf16[1024,1024]{1,0:T(8,128)(2,1)S(1)} %get-tuple-element.13) | copy-start | bytes 6291460
  220.2 11.1 %copy-start.22 = (bf16[1024,4]{0,1:T(4,128)(2,1)S(1)}, bf16[1024,4]{0,1:T(4,128)(2,1)}, u32[]{:S(2)}) copy-start(bf16[1024,4]{0,1:T(4,128)(2,1)} %param.35) | copy-start | bytes 24580
  220.2 11.9 %copy-start.24 = (bf16[1024,4]{0,1:T(4,128)(2,1)S(1)}, bf16[1024,4]{0,1:T(4,128)(2,1)}, u32[]{:S(2)}) copy-start(bf16[1024,4]{0,1:T(4,128)(2,1)} %param.37) | copy-start | bytes 24580
  240.5 54.5 %all-to-all-start.3 = ((bf16[8,1,128,1024]{3,2,1,0:T(8,128)(2,1)}), bf16[8,1,128,1024]{3,2,1,0:T(8,128)(2,1)}, u32[]{:S(2)}, u32[]{:S(2)}) async-start(bf16[8,1,128,1024]{3,2,1,0:T(8,128)(2,1)} %bitcast.76), calls=%async_computation.3 | async-start | bytes 4194304 | tf_op jit(solution)/shard_map/all_to_all | solution.py:210
  264.2 35.2 %copy-start.12 = (bf16[1024,4]{0,1:T(4,128)(2,1)S(1)}, bf16[1024,4]{0,1:T(4,128)(2,1)}, u32[]{:S(2)}) copy-start(bf16[1024,4]{0,1:T(4,128)(2,1)} %copy-done.11) | copy-start | bytes 24580
  264.2 38.0 %copy-start.10 = (bf16[1024,4]{0,1:T(4,128)(2,1)S(1)}, bf16[1024,4]{0,1:T(4,128)(2,1)}, u32[]{:S(2)}) copy-start(bf16[1024,4]{0,1:T(4,128)(2,1)} %copy-done.9) | copy-start | bytes 24580
  295.0 54.2 %all-to-all-start.1 = ((bf16[8,1,128,1024]{3,2,1,0:T(8,128)(2,1)}), bf16[8,1,128,1024]{3,2,1,0:T(8,128)(2,1)}, u32[]{:S(2)}, u32[]{:S(2)}) async-start(bf16[8,1,128,1024]{3,2,1,0:T(8,128)(2,1)} %bitcast.79), calls=%async_computation.1 | async-start | bytes 4194304 | tf_op jit(solution)/shard_map/all_to_all | solution.py:210
  299.3 138.5 %all-reduce.5.cloned.1.call-start = ((), (), s32[]{:S(2)}) async-start(), calls=%async_computation.4 | async-start | bytes 131072 | tf_op jit(solution)/shard_map/psum | solution.py:276
  (16 other events, 55.4 us)
Sparse Core Ops, SparseCore 0:
  306.9 130.8 all-reduce.4

commit v2 on v1

--- a/solution.py
+++ b/solution.py
@@ -11,6 +11,9 @@
 RANK = 4
 LANES = 128
 STEP = 256
+CHUNK = 256
+TILE = 512
+VMEM = 56 << 20
 
 
 epsilon = 1e-05
@@ -41,11 +44,18 @@
         left, right, (((1,), (1,)), ((), ())), preferred_element_type=jnp.float32
     )
 
+
 def nt(a, b):
     return lax.dot_general(a, b, (((1,), (1,)), ((), ())), preferred_element_type=jnp.float32)
 
+
 def tn(a, b):
     return lax.dot_general(a, b, (((0,), (0,)), ((), ())), preferred_element_type=jnp.float32)
+
+
+def nn(a, b):
+    return jnp.dot(a, b, preferred_element_type=jnp.float32)
+
 
 def thirds(x):
     first = x.astype(jnp.bfloat16)
@@ -54,16 +64,19 @@
     third = (rest - second.astype(jnp.float32)).astype(jnp.bfloat16)
     return first, second, third
 
+
 def lanes_of(head):
     lane = lax.broadcasted_iota(jnp.int32, (1, LANES), 1)
     own = (lane // HD) == head
     spare = lane - HD * (1 - head)
     return own, spare
 
+
 def at_spare(spare, start, parts, rest):
     for index, part in enumerate(parts):
         rest = jnp.where(spare == start + index, part, rest)
     return rest
+
 
 def forward_kernel(lengths, q_ref, k_ref, v_ref, mixed_ref, aux_ref):
     length = lengths[pl.program_id(0)]
@@ -93,6 +106,7 @@
             auxs.append(at_spare(spare[h], 1, parts, jnp.where(spare[h] == 0, one, zero)))
         mixed_ref[start:stop] = jnp.where(own[0], outs[0], outs[1]).astype(jnp.bfloat16)
         aux_ref[start:stop] = jnp.where(own[0], auxs[1], auxs[0])
+
 
 def backward_kernel(lengths, q_ref, k_ref, v_ref, mixed_ref, aux_ref, do_ref, dq_ref, dk_ref, dv_ref, acc):
     length = lengths[pl.program_id(0)]
@@ -134,8 +148,10 @@
             acc[start:] += dq
     dq_ref[...] = (acc[...] * HD ** -0.5).astype(jnp.bfloat16)
 
+
 def column(offset):
     return lambda slot, pair, lengths: (slot, offset + pair)
+
 
 def attention_forward(lengths, qkv, width):
     slots = lengths.shape[0]
@@ -152,6 +168,7 @@
         compiler_params=pltpu.CompilerParams(vmem_limit_bytes=48 << 20),
         name="attention_forward",
     )(lengths, qkv, qkv, qkv)
+
 
 def attention_backward(lengths, qkv, mixed, aux, d_mixed, width):
     slots = lengths.shape[0]
@@ -169,6 +186,184 @@
         compiler_params=pltpu.CompilerParams(vmem_limit_bytes=48 << 20),
         name="attention_backward",
     )(lengths, qkv, qkv, qkv, mixed, aux, d_mixed)
+
+
+def standardize(values):
+    centred = values - jnp.mean(values, axis=-1, keepdims=True)
+    inverse = lax.rsqrt(jnp.mean(centred * centred, axis=-1, keepdims=True) + epsilon)
+    return centred * inverse, inverse
+
+
+def pull_norm(grad, standard, inverse, gain):
+    scaled = grad * gain
+    centred = scaled - jnp.mean(scaled, axis=-1, keepdims=True)
+    return inverse * (centred - standard * jnp.mean(scaled * standard, axis=-1, keepdims=True))
+
+
+def f32(ref):
+    return ref[...].astype(jnp.float32)
+
+
+def chunks_of(rows):
+    return [pl.ds(start, CHUNK) for start in range(0, rows, CHUNK)]
+
+
+def project_kernel(tokens, gain, shift, weight, bias, downs, ups, qkv, lows, normed):
+    rows = tokens.shape[0]
+    @pl.when(pl.program_id(0) == 0)
+    def _():
+        for part in chunks_of(rows):
+            standard, _ = standardize(tokens[part].astype(jnp.float32))
+            normed[part] = (standard * f32(gain) + f32(shift)).astype(jnp.bfloat16)
+            lows[part] = nn(normed[part], downs[...]).astype(jnp.bfloat16)
+    for part in chunks_of(rows):
+        qkv[part] = (nn(normed[part], weight[...]) + bias[...] + nn(lows[part], ups[...])).astype(jnp.bfloat16)
+
+
+def project(tokens, gain, shift, weight, bias, downs, ups):
+    rows, width = tokens.shape
+    wide = weight.shape[1]
+    small = downs.shape[1]
+    fixed = lambda shape: pl.BlockSpec(shape, lambda i: (0, 0))
+    sliding = lambda depth: pl.BlockSpec((depth, TILE), lambda i: (0, i))
+    return pl.pallas_call(
+        project_kernel, grid=(wide // TILE,),
+        in_specs=[fixed((rows, width)), fixed((1, width)), fixed((1, width)), sliding(width), sliding(1), fixed((width, small)), sliding(small)],
+        out_specs=[sliding(rows), fixed((rows, small))],
+        out_shape=[jax.ShapeDtypeStruct((rows, wide), jnp.bfloat16), jax.ShapeDtypeStruct((rows, small), jnp.bfloat16)],
+        scratch_shapes=[pltpu.VMEM((rows, width), jnp.bfloat16)],
+        compiler_params=pltpu.CompilerParams(vmem_limit_bytes=VMEM),
+        name="project",
+    )(tokens, gain, shift, weight, bias, downs, ups)
+
+
+def gelu_and_slope(u):
+    c = (2.0 / jnp.pi) ** 0.5
+    square = u * u
+    share = 0.5 + 0.5 * jnp.tanh(u * (c + (c * 0.044715) * square))
+    value = u * share
+    slope = share + value * (1.0 - share) * (2 * c + (6 * c * 0.044715) * square)
+    return value, slope
+
+
+def feed_kernel(tokens, mixed, out_weight, out_bias, gain, shift, up, up_bias, down, down_bias, result, middle, slopes, total, normed):
+    rows = tokens.shape[0]
+    step = pl.program_id(0)
+    @pl.when(step == 0)
+    def _():
+        for part in chunks_of(rows):
+            m = tokens[part].astype(jnp.float32) + nn(mixed[part], out_weight[...]) + f32(out_bias)
+            middle[part] = m
+            standard, _ = standardize(m)
+            normed[part] = (standard * f32(gain) + f32(shift)).astype(jnp.bfloat16)
+            total[part] = m + f32(down_bias)
+    for part in chunks_of(rows):
+        value, slope = gelu_and_slope(nn(normed[part], up[...]) + f32(up_bias))
+        slopes[part] = slope.astype(jnp.bfloat16)
+        total[part] += nn(value.astype(jnp.bfloat16), down[...])
+    @pl.when(step == pl.num_programs(0) - 1)
+    def _():
+        result[...] = total[...].astype(jnp.bfloat16)
+
+
+def feed(tokens, mixed, out_weight, out_bias, gain, shift, up, up_bias, down, down_bias):
+    rows, width = tokens.shape
+    wide = up.shape[1]
+    fixed = lambda shape: pl.BlockSpec(shape, lambda i: (0, 0))
+    sliding = lambda depth: pl.BlockSpec((depth, TILE), lambda i: (0, i))
+    return pl.pallas_call(
+        feed_kernel, grid=(wide // TILE,),
+        in_specs=[fixed((rows, width)), fixed((rows, width)), fixed((width, width)), fixed((1, width)), fixed((1, width)), fixed((1, width)),
+                  sliding(width), sliding(1), pl.BlockSpec((TILE, width), lambda i: (i, 0)), fixed((1, width))],
+        out_specs=[fixed((rows, width)), fixed((rows, width)), sliding(rows)],
+        out_shape=[jax.ShapeDtypeStruct((rows, width), jnp.bfloat16), jax.ShapeDtypeStruct((rows, width), jnp.float32), jax.ShapeDtypeStruct((rows, wide), jnp.bfloat16)],
+        scratch_shapes=[pltpu.VMEM((rows, width), jnp.float32), pltpu.VMEM((rows, width), jnp.bfloat16)],
+        compiler_params=pltpu.CompilerParams(vmem_limit_bytes=VMEM),
+        name="feed",
+    )(tokens, mixed, out_weight, out_bias, gain, shift, up, up_bias, down, down_bias)
+
+
+def feed_back_kernel(outer, slopes, up, down, middle, gain, out_weight, d_middle, d_mixed, total):
+    rows = outer.shape[0]
+    step = pl.program_id(0)
+    for part in chunks_of(rows):
+        d_hidden = (nt(outer[part], down[...]) * slopes[part].astype(jnp.float32)).astype(jnp.bfloat16)
+        grad = nt(d_hidden, up[...])
+        @pl.when(step == 0)
+        def _():
+            total[part] = grad
+        @pl.when(step > 0)
+        def _():
+            total[part] += grad
+    @pl.when(step == pl.num_programs(0) - 1)
+    def _():
+        for part in chunks_of(rows):
+            standard, inverse = standardize(middle[part])
+            d = outer[part].astype(jnp.float32) + pull_norm(total[part], standard, inverse, f32(gain))
+            d_middle[part] = d
+            d_mixed[part] = nt(d.astype(jnp.bfloat16), out_weight[...]).astype(jnp.bfloat16)
+
+
+def feed_back(outer, slopes, up, down, middle, gain, out_weight):
+    rows, width = outer.shape
+    wide = up.shape[1]
+    fixed = lambda shape: pl.BlockSpec(shape, lambda i: (0, 0))
+    sliding = lambda depth: pl.BlockSpec((depth, TILE), lambda i: (0, i))
+    return pl.pallas_call(
+        feed_back_kernel, grid=(wide // TILE,),
+        in_specs=[fixed((rows, width)), sliding(rows), sliding(width), pl.BlockSpec((TILE, width), lambda i: (i, 0)),
+                  fixed((rows, width)), fixed((1, width)), fixed((width, width))],
+        out_specs=[fixed((rows, width)), fixed((rows, width))],
+        out_shape=[jax.ShapeDtypeStruct((rows, width), jnp.float32), jax.ShapeDtypeStruct((rows, width), jnp.bfloat16)],
+        scratch_shapes=[pltpu.VMEM((rows, width), jnp.float32)],
+        compiler_params=pltpu.CompilerParams(vmem_limit_bytes=VMEM),
+        name="feed_back",
+    )(outer, slopes, up, down, middle, gain, out_weight)
+
+
+def finish_kernel(dq, dk, dv, tokens, d_middle, lows, gain, shift, weight, downs, ups, grads, factors):
+    width = tokens.shape[1]
+    step = pl.program_id(0)
+    standard, inverse = standardize(f32(tokens))
+    normed = (standard * f32(gain) + f32(shift)).astype(jnp.bfloat16)
+    small = (nt(dq[...], ups[:, :width]) + nt(dv[...], ups[:, 2 * width:])).astype(jnp.bfloat16)
+    d_normed = nt(dq[...], weight[:, :width]) + nt(dk[...], weight[:, width:2 * width]) + nt(dv[...], weight[:, 2 * width:]) + nt(small, downs[...])
+    grads[...] = (f32(d_middle) + pull_norm(d_normed, standard, inverse, f32(gain))).astype(grads.dtype)
+    parts = [tn(small, normed), tn(lows[...], dq[...]), tn(lows[...], dv[...])]
+    @pl.when(step == 0)
+    def _():
+        for index, part in enumerate(parts):
+            factors[index] = part
+    @pl.when(step > 0)
+    def _():
+        for index, part in enumerate(parts):
+            factors[index] += part
+
+
+def finish(dq, dk, dv, tokens, d_middle, lows, gain, shift, weight, downs, ups):
+    rows, width = tokens.shape
+    small = downs.shape[1]
+    fixed = lambda shape: pl.BlockSpec(shape, lambda i: (0,) * len(shape))
+    sliding = lambda across: pl.BlockSpec((CHUNK, across), lambda i: (i, 0))
+    return pl.pallas_call(
+        finish_kernel, grid=(rows // CHUNK,),
+        in_specs=[sliding(width)] * 5 + [sliding(small), fixed((1, width)), fixed((1, width)), fixed(weight.shape), fixed(downs.shape), fixed(ups.shape)],
+        out_specs=[sliding(width), fixed((3, small, width))],
+        out_shape=[jax.ShapeDtypeStruct((rows, width), jnp.bfloat16), jax.ShapeDtypeStruct((3, small, width), jnp.float32)],
+        compiler_params=pltpu.CompilerParams(vmem_limit_bytes=VMEM),
+        name="finish",
+    )(dq, dk, dv, tokens, d_middle, lows, gain, shift, weight, downs, ups)
+
+
+def sum_over(v, axis):
+    size = lax.axis_size(axis)
+    if size & (size - 1):
+        return lax.psum(v, axis)
+    step = 1
+    while step < size:
+        v = v + lax.ppermute(v, axis, [(i, i ^ step) for i in range(size)])
+        step *= 2
+    return v
 
 
 def whole_slots(
@@ -200,83 +395,84 @@
     positions = slots * rows * ranks
 
     def to_slots(v):
-        pieces = lax.all_to_all(
-            v.reshape(ranks, slots, rows, width), "blk", 0, 0, tiled=True
-        )
+        pieces = lax.all_to_all(v.reshape(ranks, slots, rows, width), "blk", 0, 0, tiled=True)
         return jnp.swapaxes(pieces, 0, 1).reshape(positions, width)
 
     def to_rows(v):
         pieces = jnp.swapaxes(v.reshape(slots, ranks, rows, width), 0, 1)
         return lax.all_to_all(pieces, "blk", 0, 0, tiled=True).reshape(seqs_here, rows, width)
 
+    def line(v):
+        return v.reshape(1, -1)
+
     my_lengths = lax.dynamic_slice_in_dim(lengths, lax.axis_index("blk") * slots, slots)
-    flat = to_slots(tokens).astype(jnp.float32)
+    bias = line(jnp.concatenate((query_bias, jnp.zeros_like(query_bias), value_bias)))
+    downs = jnp.pad(
+        jnp.concatenate((query_down, value_down), axis=1), ((0, 0), (0, LANES - 2 * RANK))
+    )
+    ups = adapter * (
+        jnp.pad(query_up, ((0, LANES - RANK), (0, 2 * width)))
+        + jnp.pad(value_up, ((RANK, LANES - 2 * RANK), (2 * width, 0)))
+    )
+    ups = ups.astype(jnp.bfloat16)
+    inner = to_slots(tokens)
     outer = to_slots(cotangent)
-    normed_full, standard, inverse = normalize(flat, norm_gain, norm_shift)
-    normed = normed_full.astype(jnp.bfloat16)
-    joint = jnp.dot(normed, joint_weight, preferred_element_type=jnp.float32)
-    query_low = jnp.dot(normed, query_down, preferred_element_type=jnp.float32).astype(jnp.bfloat16)
-    value_low = jnp.dot(normed, value_down, preferred_element_type=jnp.float32).astype(jnp.bfloat16)
-    bias = jnp.concatenate((query_bias, jnp.zeros_like(query_bias), value_bias)).astype(jnp.float32)
-    lows = jnp.concatenate((query_low, value_low), axis=1)
-    nothing = jnp.zeros_like(query_up)
-    ups = jnp.concatenate(
+    qkv, lows = project(
+        inner, line(norm_gain), line(norm_shift), joint_weight, bias, downs, ups
+    )
+    mixed, aux = attention_forward(my_lengths, qkv, width)
+    result, middle, slopes = feed(
+        inner,
+        mixed,
+        output_weight,
+        line(output_bias),
+        line(second_gain),
+        line(second_shift),
+        upward_weight,
+        line(upward_bias),
+        down_weight,
+        line(down_bias),
+    )
+    result, middle, slopes, outer = lax.optimization_barrier((result, middle, slopes, outer))
+    block_output = to_rows(result)
+    d_middle, d_mixed = feed_back(
+        outer, slopes, upward_weight, down_weight, middle, line(second_gain), output_weight
+    )
+    d_queries, d_keys, d_values = attention_backward(
+        my_lengths, qkv, mixed, aux, d_mixed, width
+    )
+    grads, factors = finish(
+        d_queries,
+        d_keys,
+        d_values,
+        inner,
+        d_middle,
+        lows,
+        line(norm_gain),
+        line(norm_shift),
+        joint_weight,
+        downs,
+        ups,
+    )
+    token_grads = to_rows(grads).astype(jnp.float32)
+    packed = jnp.concatenate(
         (
-            jnp.concatenate((query_up, nothing, nothing), axis=1),
-            jnp.concatenate((nothing, nothing, value_up), axis=1),
-        ),
-        axis=0,
-    )
-    qkv = (
-        joint + bias + adapter * jnp.dot(lows, ups, preferred_element_type=jnp.float32)
-    ).astype(jnp.bfloat16)
-    mixed, aux = attention_forward(my_lengths, qkv, width)
-    middle = (
-        flat
-        + jnp.dot(mixed, output_weight, preferred_element_type=jnp.float32)
-        + output_bias.astype(jnp.float32)
-    )
-    normed_two_full, standard_two, inverse_two = normalize(middle, second_gain, second_shift)
-    normed_two = normed_two_full.astype(jnp.bfloat16)
-    hidden = jnp.dot(
-        normed_two, upward_weight, preferred_element_type=jnp.float32
-    ) + upward_bias.astype(jnp.float32)
-    active_full, gelu_pull = jax.vjp(partial(jax.nn.gelu, approximate=True), hidden)
-    active = active_full.astype(jnp.bfloat16)
-    block_output = (
-        middle
-        + jnp.dot(active, down_weight, preferred_element_type=jnp.float32)
-        + down_bias.astype(jnp.float32)
-    ).astype(jnp.bfloat16)
-    block_output = to_rows(block_output)
-    d_active = against(outer, down_weight)
-    d_hidden = gelu_pull(d_active)[0].astype(jnp.bfloat16)
-    d_normed_two = against(d_hidden, upward_weight)
-    d_middle = outer.astype(jnp.float32) + norm_back(
-        d_normed_two, standard_two, inverse_two, second_gain
-    )
-    d_mixed = against(d_middle.astype(jnp.bfloat16), output_weight).astype(jnp.bfloat16)
-    d_query_low, d_key_low, d_value_low = attention_backward(
-        my_lengths, qkv, mixed, aux, d_mixed, width
-    )
-    query_up_grad = adapter * transposed(query_low, d_query_low)
-    value_up_grad = adapter * transposed(value_low, d_value_low)
-    d_query_small = (adapter * against(d_query_low, query_up)).astype(jnp.bfloat16)
-    d_value_small = (adapter * against(d_value_low, value_up)).astype(jnp.bfloat16)
-    query_down_grad = transposed(normed, d_query_small)
-    value_down_grad = transposed(normed, d_value_small)
-    d_joint = jnp.concatenate((d_query_low, d_key_low, d_value_low), axis=1)
-    d_normed = (
-        against(d_joint, joint_weight)
-        + against(d_query_small, query_down)
-        + against(d_value_small, value_down)
-    )
-    token_grads = d_middle + norm_back(d_normed, standard, inverse, norm_gain)
-    token_grads = to_rows(token_grads.astype(jnp.bfloat16)).astype(jnp.float32)
-    sums = lax.psum(
-        (query_down_grad, query_up_grad, value_down_grad, value_up_grad), ("batch", "blk")
-    )
-    return (block_output, token_grads, sums[0], sums[1], sums[2], sums[3])
+            factors[0, : 2 * RANK],
+            adapter * factors[1, :RANK],
+            adapter * factors[2, RANK : 2 * RANK],
+        )
+    )
+    packed = sum_over(sum_over(packed, "batch"), "blk")
+    query_down_grad, value_down_grad = packed[:RANK].T, packed[RANK : 2 * RANK].T
+    query_up_grad, value_up_grad = packed[2 * RANK : 3 * RANK], packed[3 * RANK :]
+    return (
+        block_output,
+        token_grads,
+        query_down_grad,
+        query_up_grad,
+        value_down_grad,
+        value_up_grad,
+    )
 
 
 def body(

time: 460 us -> 322 us (0.70); the launches traced: 450 us -> 321 us
  waiting for transfers between devices: 206 us -> 40.6 us
  matrix products: 111 us -> 0 us
  Pallas kernels: 68.4 us -> 179 us
  blocking collectives: 0 us -> 55.5 us
  other arithmetic: 20 us -> 4.32 us
  between operations: 14.9 us -> 0.85 us
  local copies, waits for them, and re-layouts: 9.27 us -> 17.6 us
    dot_general x18 -> x0, matrix products: 111 us -> none  [the longest x7 55.1 us: against(): lax.dot_general(left, right, (((1,), (1,)), ((), ())), preferred_element_...]
    pallas_call x0 -> x4, Pallas kernels: none -> 111 us  [the longest x1 41 us: feed_back(): pl.pallas_call(feed_back_kernel, grid=(wide // TILE,), in_specs=[fixed((r...]
    psum x1 -> x0, waiting for transfers between devices: 88.7 us -> none  [whole_slots(): lax.psum((query_down_grad, query_up_grad, value_down_grad, value_up_grad)...]
    all_to_all x2, waiting for transfers between devices: 69.1 us -> 0.01 us  [to_rows(): lax.all_to_all(pieces, 'blk', 0, 0, tiled=True)]
    all_to_all x0 -> x1, blocking collectives: none -> 55.5 us  [to_slots(): lax.all_to_all(v.reshape(ranks, slots, rows, width), 'blk', 0, 0, tiled=T...]
    all_to_all x2 -> x1, waiting for transfers between devices: 48.3 us -> 0.01 us  [to_slots(): lax.all_to_all(v.reshape(ranks, slots, rows, width), 'blk', 0, 0, tiled=T...]
    ppermute x0 -> x5, waiting for transfers between devices: none -> 40.6 us  [sum_over(): v = v + lax.ppermute(v, axis, [(i, i ^ step) for i in range(size)])]
    ppermute x0 -> x5, starting transfers between devices: none -> 9.64 us  [sum_over(): v = v + lax.ppermute(v, axis, [(i, i ^ step) for i in range(size)])]
  transfers between devices with their start and end apart: 5 -> 8, of which waited for: 4 -> 5; matrix products, arithmetic and copies ran while one was open for 15% -> 3% of each run, Pallas kernels for 7% -> 56%
where the time goes in v2:
time: 322 us; the launch traced here: 321 us
  Pallas kernels  179 us (56%)
  blocking collectives  55.5 us (17%)
  waiting for transfers between devices  40.6 us (13%)
  starting transfers between devices  23.5 us (7%)
  local copies, waits for them, and re-layouts  17.6 us (5%)
  other arithmetic  4.32 us (1%)
    all_to_all x1, blocking collectives, to_slots(): lax.all_to_all(v.reshape(ranks, slots, rows, width), 'blk', 0, 0, tiled=T...  55.5 us
    pallas_call x1, Pallas kernels, feed_back(): pl.pallas_call(feed_back_kernel, grid=(wide // TILE,), in_specs=[fixed((r...  41 us
    ppermute x5, waiting for transfers between devices, sum_over(): v = v + lax.ppermute(v, axis, [(i, i ^ step) for i in range(size)])  40.6 us
    pallas_call x1, Pallas kernels, feed(): pl.pallas_call(feed_kernel, grid=(wide // TILE,), in_specs=[fixed((rows,...  37.8 us
    pallas_call x1, Pallas kernels, attention_backward(): pl.pallas_call(backward_kernel, grid_spec=pltpu.PrefetchScalarGridSpec(nu...  36.6 us
    pallas_call x1, Pallas kernels, attention_forward(): pl.pallas_call(forward_kernel, grid_spec=pltpu.PrefetchScalarGridSpec(num...  31.3 us
    pallas_call x1, Pallas kernels, finish(): pl.pallas_call(finish_kernel, grid=(rows // CHUNK,), in_specs=[sliding(wi...  17.5 us
    pallas_call x1, Pallas kernels, project(): pl.pallas_call(project_kernel, grid=(wide // TILE,), in_specs=[fixed((row...  14.4 us
  transfers between devices with their start and end apart: 8, of which 5 were waited for; matrix products, arithmetic and copies ran while one was open for 3% of the time, Pallas kernels for 56%

profile of v2, /device:TPU:0, one launch (start us, length us, event | category | flops | bytes accessed | tf_op | source)
XLA Modules:
  0.0 321.0 jit_solution(12108198075213028970)
XLA Ops:
  0.6 55.5 %all_to_all.20 = bf16[8,1,128,1024]{3,2,1,0:T(8,128)(2,1)} all-to-all(bf16[8,1,128,1024]{3,2,1,0:T(8,128)(2,1)} %bitcast.28), channel_id=1, replica_groups=mesh['batch'=4,'blk'=8] {'blk'}, dimensions={0} | all-to-all | bytes 4194304 | tf_op jit(solution)/shard_map/all_to_all | solution.py:398
  56.3 3.7 %all-to-all-start.1 = ((bf16[8,1,128,1024]{3,2,1,0:T(8,128)(2,1)}), bf16[8,1,128,1024]{3,2,1,0:T(8,128)(2,1)S(1)}, u32[]{:S(2)}, u32[]{:S(2)}) async-start(bf16[8,1,128,1024]{3,2,1,0:T(8,128)(2,1)} %bitcast.29), calls=%async_computation.1 | async-start | bytes 4194304 | tf_op jit(solution)/shard_map/all_to_all | solution.py:398
  65.1 0.8 pad.12.downs
  65.8 0.6 dynamic_slice.3.lengths
  66.5 1.0 add_multiply_fusion.ups
  67.5 14.4 %project.1 = (bf16[1024,3072]{1,0:T(8,128)(2,1)}, bf16[1024,128]{1,0:T(8,128)(2,1)}) custom-call(bf16[1024,1024]{1,0:T(8,128)(2,1)} %bitcast.24, bf16[1,1024]{1,0:T(2,128)(2,1)} %reshape.56.gain, bf16[1,1024]{1,0:T(2,128)(2,1)} %reshape.57.shift, bf16[1024,3072]{1,0:T(8,128)(2,1)} %weight.3, bf16[1,3072]{1,0:T(2,128)(2,1)} %reshape.58.bias, ...), custom_call_target="tpu_custom_call" | custom-call | tf_op jit(solution)/shard_map/project/pallas_call | solution.py:229
  81.9 31.3 %attention_forward.1 = (bf16[1024,1024]{1,0:T(8,128)(2,1)S(1)}, bf16[1024,1024]{1,0:T(8,128)(2,1)S(1)}) custom-call(s32[1]{0:T(128)} %dynamic_slice.3.lengths, bf16[1024,3072]{1,0:T(8,128)(2,1)} %get-tuple-element.24.q_ref.k_ref.v_ref, bf16[1024,3072]{1,0:T(8,128)(2,1)} %get-tuple-element.24.q_ref.k_ref.v_ref, ...), custom_call_target="tpu_custom_call" | custom-call | tf_op jit(solution)/shard_map/attention_forward/pallas_call | solution.py:161
  113.2 1.3 copy-done
  114.5 1.4 copy-done.3
  115.9 37.8 %feed.1 = (bf16[1024,1024]{1,0:T(8,128)(2,1)}, f32[1024,1024]{1,0:T(8,128)}, bf16[1024,4096]{1,0:T(8,128)(2,1)}) custom-call(bf16[1024,1024]{1,0:T(8,128)(2,1)} %bitcast.25, bf16[1024,1024]{1,0:T(8,128)(2,1)} %copy-done, bf16[1024,1024]{1,0:T(8,128)(2,1)} %out_weight.3, bf16[1,1024]{1,0:T(2,128)(2,1)} %reshape.59.out_bias, bf16[1,1024]{1,0:T(2,128)(2,1)} %reshape.60.gain, ...), custom_call_target="tpu_custom_call" | custom-call | tf_op jit(solution)/shard_map/feed/pallas_call | solution.py:274
  153.7 1.3 copy-done.4
  155.0 5.0 %all-to-all-start.2 = ((bf16[8,1,128,1024]{3,2,1,0:T(8,128)(2,1)}), bf16[8,1,128,1024]{3,2,1,0:T(8,128)(2,1)}, u32[]{:S(2)}, u32[]{:S(2)}) async-start(bf16[8,1,128,1024]{3,2,1,0:T(8,128)(2,1)} %bitcast.31), calls=%async_computation.2 | async-start | bytes 4194304 | tf_op jit(solution)/shard_map/all_to_all | solution.py:403
  160.0 41.0 %feed_back.1 = (f32[1024,1024]{1,0:T(8,128)}, bf16[1024,1024]{1,0:T(8,128)(2,1)}) custom-call(bf16[1024,1024]{1,0:T(8,128)(2,1)} %bitcast.27, bf16[1024,4096]{1,0:T(8,128)(2,1)} %get-tuple-element.32.slopes, bf16[1024,4096]{1,0:T(8,128)(2,1)} %up.3, bf16[4096,1024]{1,0:T(8,128)(2,1)} %down.3, f32[1024,1024]{1,0:T(8,128)} %get-tuple-element.33.middle, ...), custom_call_target="tpu_custom_call" | custom-call | tf_op jit(solution)/shard_map/feed_back/pallas_call | solution.py:312
  201.0 36.6 %attention_backward.1 = (bf16[1024,1024]{1,0:T(8,128)(2,1)S(1)}, bf16[1024,1024]{1,0:T(8,128)(2,1)S(1)}, bf16[1024,1024]{1,0:T(8,128)(2,1)}) custom-call(s32[1]{0:T(128)} %dynamic_slice.3.lengths, bf16[1024,3072]{1,0:T(8,128)(2,1)} %get-tuple-element.24.q_ref.k_ref.v_ref, bf16[1024,3072]{1,0:T(8,128)(2,1)} %get-tuple-element.24.q_ref.k_ref.v_ref, ...), custom_call_target="tpu_custom_call" | custom-call | tf_op jit(solution)/shard_map/attention_backward/pallas_call | solution.py:178
  237.6 1.3 copy-done.1
  239.0 1.3 copy-done.2
  240.3 17.5 %finish.1 = (bf16[1024,1024]{1,0:T(8,128)(2,1)}, f32[3,128,1024]{2,1,0:T(8,128)}) custom-call(bf16[1024,1024]{1,0:T(8,128)(2,1)} %copy-done.1, bf16[1024,1024]{1,0:T(8,128)(2,1)} %copy-done.2, bf16[1024,1024]{1,0:T(8,128)(2,1)} %get-tuple-element.37.dv, bf16[1024,1024]{1,0:T(8,128)(2,1)} %bitcast.26, f32[1024,1024]{1,0:T(8,128)} %get-tuple-element.38.d_middle, ...), custom_call_target="tpu_custom_call" | custom-call | tf_op jit(solution)/shard_map/finish/pallas_call | solution.py:348
  257.8 5.1 %all-to-all-start.3 = ((bf16[8,1,128,1024]{3,2,1,0:T(8,128)(2,1)}), bf16[8,1,128,1024]{3,2,1,0:T(8,128)(2,1)S(1)}, u32[]{:S(2)}, u32[]{:S(2)}) async-start(bf16[8,1,128,1024]{3,2,1,0:T(8,128)(2,1)} %bitcast.30), calls=%async_computation.3 | async-start | bytes 4194304 | tf_op jit(solution)/shard_map/all_to_all | solution.py:403
  262.9 0.8 slice_bitcast_fusion
  263.7 0.8 multiply_bitcast_fusion.1
  264.5 1.6 collective-permute-start
  266.0 3.0 collective-permute-done
  269.1 1.6 collective-permute-start.1
  270.6 2.7 collective-permute-done.1
  273.5 1.2 collective-permute-done.2
  274.7 1.8 collective-permute-start.3
  276.6 22.6 %collective-permute-done.3 = f32[16,1024]{1,0:T(8,128)S(1)} collective-permute-done((f32[16,1024]{1,0:T(8,128)S(1)}, f32[16,1024]{1,0:T(8,128)S(1)}, u32[]{:S(2)}, u32[]{:S(2)}) %collective-permute-start.3) | collective-permute-done | bytes 65568 | tf_op jit(solution)/shard_map/ppermute | solution.py:364
  299.2 4.6 %collective-permute-start.4 = (f32[16,1024]{1,0:T(8,128)S(1)}, f32[16,1024]{1,0:T(8,128)S(1)}, u32[]{:S(2)}, u32[]{:S(2)}) collective-permute-start(f32[16,1024]{1,0:T(8,128)S(1)} %add.32), channel_id=1, source_target_pairs={{0,4},{1,5},{2,6},{3,7},{4,0},{5,1},{6,2},{7,3},{8,12},{9,13},{10,... | collective-permute-start | bytes 196616 | tf_op jit(solution)/shard_map/ppermute | solution.py:364
  303.8 11.0 %collective-permute-done.4 = f32[16,1024]{1,0:T(8,128)S(1)} collective-permute-done((f32[16,1024]{1,0:T(8,128)S(1)}, f32[16,1024]{1,0:T(8,128)S(1)}, u32[]{:S(2)}, u32[]{:S(2)}) %collective-permute-start.4) | collective-permute-done | bytes 65568 | tf_op jit(solution)/shard_map/ppermute | solution.py:364
  314.8 0.6 fusion.1
  315.4 2.5 bitcast_convert_fusion
  317.9 3.1 copy.32
  (55 shorter events, 5.2 us)
Async XLA Ops:
  56.1 3.9 %copy-start.10 = (bf16[1024]{0:T(1024)(128)(2,1)S(1)}, bf16[1024]{0:T(1024)(128)(2,1)}, u32[]{:S(2)}) copy-start(bf16[1024]{0:T(1024)(128)(2,1)} %param.22) | copy-start | bytes 6148
  56.1 4.5 %copy-start.11 = (bf16[1024]{0:T(1024)(128)(2,1)S(1)}, bf16[1024]{0:T(1024)(128)(2,1)}, u32[]{:S(2)}) copy-start(bf16[1024]{0:T(1024)(128)(2,1)} %param.23) | copy-start | bytes 6148
  56.1 5.1 %copy-start.12 = (bf16[1024]{0:T(1024)(128)(2,1)S(1)}, bf16[1024]{0:T(1024)(128)(2,1)}, u32[]{:S(2)}) copy-start(bf16[1024]{0:T(1024)(128)(2,1)} %param.29) | copy-start | bytes 6148
  56.1 5.7 %copy-start.13 = (bf16[1024]{0:T(1024)(128)(2,1)S(1)}, bf16[1024]{0:T(1024)(128)(2,1)}, u32[]{:S(2)}) copy-start(bf16[1024]{0:T(1024)(128)(2,1)} %param.28) | copy-start | bytes 6148
  56.1 6.3 %copy-start.14 = (bf16[1024]{0:T(1024)(128)(2,1)S(1)}, bf16[1024]{0:T(1024)(128)(2,1)}, u32[]{:S(2)}) copy-start(bf16[1024]{0:T(1024)(128)(2,1)} %param.30) | copy-start | bytes 6148
  56.2 6.9 %copy-start.15 = (bf16[1024]{0:T(1024)(128)(2,1)S(1)}, bf16[1024]{0:T(1024)(128)(2,1)}, u32[]{:S(2)}) copy-start(bf16[1024]{0:T(1024)(128)(2,1)} %param.34) | copy-start | bytes 6148
  56.2 7.5 %copy-start.16 = (bf16[1024]{0:T(1024)(128)(2,1)S(1)}, bf16[1024]{0:T(1024)(128)(2,1)}, u32[]{:S(2)}) copy-start(bf16[1024]{0:T(1024)(128)(2,1)} %param.26) | copy-start | bytes 6148
  56.2 7.4 %copy-start.17 = (bf16[1024]{0:T(1024)(128)(2,1)S(1)}, bf16[1024]{0:T(1024)(128)(2,1)}, u32[]{:S(2)}) copy-start(bf16[1024]{0:T(1024)(128)(2,1)} %param.25) | copy-start | bytes 6148
  56.2 8.1 %copy-start.7 = (bf16[4096]{0:T(1024)(128)(2,1)S(1)}, bf16[4096]{0:T(1024)(128)(2,1)}, u32[]{:S(2)}) copy-start(bf16[4096]{0:T(1024)(128)(2,1)} %param.32) | copy-start | bytes 24580
  56.2 8.7 %copy-start.8 = (bf16[1024,4]{0,1:T(4,128)(2,1)S(1)}, bf16[1024,4]{0,1:T(4,128)(2,1)}, u32[]{:S(2)}) copy-start(bf16[1024,4]{0,1:T(4,128)(2,1)} %param.37) | copy-start | bytes 24580
  56.2 8.7 %copy-start.9 = (bf16[1024,4]{0,1:T(4,128)(2,1)S(1)}, bf16[1024,4]{0,1:T(4,128)(2,1)}, u32[]{:S(2)}) copy-start(bf16[1024,4]{0,1:T(4,128)(2,1)} %param.35) | copy-start | bytes 24580
  56.2 9.6 %copy-start.18 = (s32[8]{0:T(128)S(1)}, s32[8]{0:T(128)}, u32[]{:S(2)}) copy-start(s32[8]{0:T(128)} %param.21) | copy-start | bytes 100
  56.2 10.2 %copy-start.5 = (bf16[4,1024]{1,0:T(4,128)(2,1)S(1)}, bf16[4,1024]{1,0:T(4,128)(2,1)}, u32[]{:S(2)}) copy-start(bf16[4,1024]{1,0:T(4,128)(2,1)} %param.38) | copy-start | bytes 24580
  56.3 10.2 %copy-start.6 = (bf16[4,1024]{1,0:T(4,128)(2,1)S(1)}, bf16[4,1024]{1,0:T(4,128)(2,1)}, u32[]{:S(2)}) copy-start(bf16[4,1024]{1,0:T(4,128)(2,1)} %param.36) | copy-start | bytes 24580
  56.3 97.4 %all-to-all-start.1 = ((bf16[8,1,128,1024]{3,2,1,0:T(8,128)(2,1)}), bf16[8,1,128,1024]{3,2,1,0:T(8,128)(2,1)S(1)}, u32[]{:S(2)}, u32[]{:S(2)}) async-start(bf16[8,1,128,1024]{3,2,1,0:T(8,128)(2,1)} %bitcast.29), calls=%async_computation.1 | async-start | bytes 4194304 | tf_op jit(solution)/shard_map/all_to_all | solution.py:398
  113.2 1.3 copy-start
  114.5 1.4 copy-start.3
  153.7 1.3 copy-start.4
  155.0 102.8 %all-to-all-start.2 = ((bf16[8,1,128,1024]{3,2,1,0:T(8,128)(2,1)}), bf16[8,1,128,1024]{3,2,1,0:T(8,128)(2,1)}, u32[]{:S(2)}, u32[]{:S(2)}) async-start(bf16[8,1,128,1024]{3,2,1,0:T(8,128)(2,1)} %bitcast.31), calls=%async_computation.2 | async-start | bytes 4194304 | tf_op jit(solution)/shard_map/all_to_all | solution.py:403
  237.6 1.3 copy-start.1
  239.0 1.3 copy-start.2
  257.8 57.6 %all-to-all-start.3 = ((bf16[8,1,128,1024]{3,2,1,0:T(8,128)(2,1)}), bf16[8,1,128,1024]{3,2,1,0:T(8,128)(2,1)S(1)}, u32[]{:S(2)}, u32[]{:S(2)}) async-start(bf16[8,1,128,1024]{3,2,1,0:T(8,128)(2,1)} %bitcast.30), calls=%async_computation.3 | async-start | bytes 4194304 | tf_op jit(solution)/shard_map/all_to_all | solution.py:403
  264.5 4.6 %collective-permute-start = (f32[16,1024]{1,0:T(8,128)S(1)}, f32[16,1024]{1,0:T(8,128)S(1)}, u32[]{:S(2)}, u32[]{:S(2)}) collective-permute-start(f32[16,1024]{1,0:T(8,128)S(1)} %pad_maximum_fusion), channel_id=1, source_target_pairs={{0,8},{8,0},{16,24},{24,16},{1,9},{9,1},{17,25},{25,17},{2,10},{10... | collective-permute-start | bytes 196616 | tf_op jit(solution)/shard_map/ppermute | solution.py:364
  269.1 4.3 %collective-permute-start.1 = (f32[16,1024]{1,0:T(8,128)S(1)}, f32[16,1024]{1,0:T(8,128)S(1)}, u32[]{:S(2)}, u32[]{:S(2)}) collective-permute-start(f32[16,1024]{1,0:T(8,128)S(1)} %fusion), channel_id=1, source_target_pairs={{0,16},{8,24},{16,0},{24,8},{1,17},{9,25},{17,1},{25,9},{2,18},{10... | collective-permute-start | bytes 196616 | tf_op jit(solution)/shard_map/ppermute | solution.py:364
  273.4 1.3 collective-permute-start.2
  274.7 24.4 %collective-permute-start.3 = (f32[16,1024]{1,0:T(8,128)S(1)}, f32[16,1024]{1,0:T(8,128)S(1)}, u32[]{:S(2)}, u32[]{:S(2)}) collective-permute-start(f32[16,1024]{1,0:T(8,128)S(1)} %add.31), channel_id=1, source_target_pairs={{0,2},{1,3},{2,0},{3,1},{4,6},{5,7},{6,4},{7,5},{8,10},{9,11},{10,... | collective-permute-start | bytes 196616 | tf_op jit(solution)/shard_map/ppermute | solution.py:364
  299.2 15.6 %collective-permute-start.4 = (f32[16,1024]{1,0:T(8,128)S(1)}, f32[16,1024]{1,0:T(8,128)S(1)}, u32[]{:S(2)}, u32[]{:S(2)}) collective-permute-start(f32[16,1024]{1,0:T(8,128)S(1)} %add.32), channel_id=1, source_target_pairs={{0,4},{1,5},{2,6},{3,7},{4,0},{5,1},{6,2},{7,3},{8,12},{9,13},{10,... | collective-permute-start | bytes 196616 | tf_op jit(solution)/shard_map/ppermute | solution.py:364

commit v3 on v0

--- a/solution.py
+++ b/solution.py
@@ -3,10 +3,27 @@
 import jax
 import jax.numpy as jnp
 from jax import lax
+from jax.experimental import pallas as pl
+from jax.experimental.pallas import tpu as pltpu
 from jax.sharding import PartitionSpec as P
 
 HD = 64
 RANK = 4
+LANES = 128
+STEP = 256
+SAFE = 80.0
+GROUP = 2
+CHUNK = 512
+TILE = 1024
+VMEM = 58 << 20
+GAIN = 0
+SHIFT = 1
+JOINT = 2
+OUT = 5
+GAIN_TWO = 6
+SHIFT_TWO = 7
+DOWN = 8
+UP = 9
 
 
 epsilon = 1e-05
@@ -35,6 +52,521 @@
 def against(left, right):
     return lax.dot_general(
         left, right, (((1,), (1,)), ((), ())), preferred_element_type=jnp.float32
+    )
+
+
+def nt(a, b):
+    return lax.dot_general(a, b, (((1,), (1,)), ((), ())), preferred_element_type=jnp.float32)
+
+
+def tn(a, b):
+    return lax.dot_general(a, b, (((0,), (0,)), ((), ())), preferred_element_type=jnp.float32)
+
+
+def nn(a, b):
+    return jnp.dot(a, b, preferred_element_type=jnp.float32)
+
+
+def thirds(x):
+    first = x.astype(jnp.bfloat16)
+    rest = x - first.astype(jnp.float32)
+    second = rest.astype(jnp.bfloat16)
+    third = (rest - second.astype(jnp.float32)).astype(jnp.bfloat16)
+    return first, second, third
+
+
+def in_first_head():
+    return lax.broadcasted_iota(jnp.int32, (1, LANES), 1) < HD
+
+
+def spare_lane():
+    return lax.broadcasted_iota(jnp.int32, (1, LANES), 1) % HD
+
+
+def key_extras(rows, length):
+    place = lax.broadcasted_iota(jnp.int32, (rows, LANES), 0)
+    bias = jnp.where(place < length, 0.0, masked_value).astype(jnp.bfloat16)
+    spare = spare_lane()
+    return jnp.where(spare == 0, bias, jnp.where(spare < 4, jnp.bfloat16(1), jnp.bfloat16(0)))
+
+
+def forward_kernel(lengths, peaks, q_ref, k_ref, v_ref, mixed_ref, aux_ref, calm):
+    group, rows = q_ref.shape[:2]
+    one, zero = jnp.bfloat16(1), jnp.bfloat16(0)
+
+    @pl.when(pl.program_id(1) == 0)
+    def _():
+        bound = jnp.max(peaks[0]) * jnp.max(peaks[1])
+        calm[0] = (bound < (SAFE / HD ** -0.5) ** 2).astype(jnp.int32)
+
+    first, spare = in_first_head(), spare_lane()
+    extras = key_extras(rows, lengths[pl.program_id(0)])
+    lead = jnp.where(spare == 0, one, zero)
+    causal = lax.broadcasted_iota(jnp.int32, (STEP, STEP), 1) <= lax.broadcasted_iota(jnp.int32, (STEP, STEP), 0)
+
+    def widen(pair):
+        q, k, v = q_ref[pair] * jnp.bfloat16(HD ** -0.5), k_ref[pair], v_ref[pair]
+        q_aug = [jnp.where(first, q, lead), jnp.where(first, lead, q)]
+        k_aug = [jnp.where(first, k, extras), jnp.where(first, extras, k)]
+        v_aug = [jnp.where(first, v, one), jnp.where(first, one, v)]
+        return q_aug, k_aug, v_aug
+
+    def write(pair, start, sums, tops):
+        total = jnp.where(first, sums[1], sums[0])
+        mixed = jnp.where(first, sums[0], sums[1]) * pltpu.roll(1.0 / total, HD, 1)
+        mixed_ref[pair, start:start + STEP] = mixed.astype(jnp.bfloat16)
+        level = jnp.log(total)
+        if tops is not None:
+            level = level + jnp.where(first, tops[1], tops[0])
+        aux = lead
+        for index, part in enumerate(thirds(-level)):
+            aux = jnp.where(spare == index + 1, part, aux)
+        aux_ref[pair, start:start + STEP] = aux
+
+    @pl.when(calm[0] == 1)
+    def _():
+        ready = widen(0)
+        for pair in range(group):
+            q_aug, k_aug, v_aug = ready
+            sums = [[None] * (rows // STEP) for _ in range(2)]
+            for start in range(0, rows, STEP):
+                stop = start + STEP
+                for h in range(2):
+                    s = nt(q_aug[h][start:], k_aug[h][start:stop])
+                    w = jnp.exp(jnp.where(causal, s[:STEP], masked_value)).astype(jnp.bfloat16)
+                    if stop < rows:
+                        w = jnp.concatenate([w, jnp.exp(s[STEP:]).astype(jnp.bfloat16)], axis=0)
+                    o = nn(w, v_aug[h][start:stop])
+                    for part in range(start // STEP, rows // STEP):
+                        add = o[part * STEP - start:(part + 1) * STEP - start]
+                        sums[h][part] = add if start == 0 else sums[h][part] + add
+                if start == 0 and pair + 1 < group:
+                    ready = widen(pair + 1)
+                write(pair, start, [sums[0][start // STEP], sums[1][start // STEP]], None)
+
+    @pl.when(calm[0] == 0)
+    def _():
+        for pair in range(group):
+            q_aug, k_aug, v_aug = widen(pair)
+            for start in range(0, rows, STEP):
+                stop = start + STEP
+                sums, tops = [], []
+                for h in range(2):
+                    s = nt(q_aug[h][start:stop], k_aug[h][:stop])
+                    edge = jnp.where(causal, s[:, start:], masked_value)
+                    s = edge if start == 0 else jnp.concatenate([s[:, :start], edge], axis=1)
+                    tops.append(jnp.max(s, axis=1, keepdims=True))
+                    w = jnp.exp(s - tops[h]).astype(jnp.bfloat16)
+                    sums.append(nn(w, v_aug[h][:stop]))
+                write(pair, start, sums, tops)
+
+
+def backward_kernel(lengths, q_ref, k_ref, v_ref, mixed_ref, aux_ref, do_ref, dq_ref, dk_ref, dv_ref, acc):
+    group, rows = q_ref.shape[:2]
+    one, zero = jnp.bfloat16(1), jnp.bfloat16(0)
+    first, spare = in_first_head(), spare_lane()
+    extras = key_extras(rows, lengths[pl.program_id(0)])
+    three = jnp.where(spare < 3, one, zero)
+    causal = lax.broadcasted_iota(jnp.int32, (STEP, STEP), 0) <= lax.broadcasted_iota(jnp.int32, (STEP, STEP), 1)
+    row = lax.broadcasted_iota(jnp.int32, (LANES, LANES), 0) // HD
+    column = lax.broadcasted_iota(jnp.int32, (LANES, LANES), 1) // HD
+    cross = jnp.where(row != column, one, zero)
+
+    def widen(pair):
+        q, k, v = q_ref[pair] * jnp.bfloat16(HD ** -0.5), k_ref[pair], v_ref[pair]
+        do, aux = do_ref[pair], aux_ref[pair]
+        k_aug = [jnp.where(first, k, extras), jnp.where(first, extras, k)]
+        q_aug = [jnp.where(first, q, aux), jnp.where(first, aux, q)]
+        v_aug = [jnp.where(first, v, three), jnp.where(first, three, v)]
+        product = do.astype(jnp.float32) * mixed_ref[pair].astype(jnp.float32)
+        high = product.astype(jnp.bfloat16)
+        low = (product - high.astype(jnp.float32)).astype(jnp.bfloat16)
+        delta = nn(high, cross) + nn(low, cross)
+        extra = zero
+        for index, part in enumerate(thirds(-delta)):
+            extra = jnp.where(spare == index, part, extra)
+        do_aug = [jnp.where(first, do, extra), jnp.where(first, extra, do)]
+        return q, k, do, q_aug, k_aug, v_aug, do_aug
+
+    ready = widen(0)
+    for pair in range(group):
+        q, k, do, q_aug, k_aug, v_aug, do_aug = ready
+        for start in range(0, rows, STEP):
+            stop = start + STEP
+            dks, dvs, dqs = [], [], []
+            for h in range(2):
+                s = nt(k_aug[h][start:stop], q_aug[h][start:])
+                edge = jnp.where(causal, s[:, :STEP], masked_value)
+                s = edge if stop == rows else jnp.concatenate([edge, s[:, STEP:]], axis=1)
+                p = jnp.exp(s)
+                dp = nt(v_aug[h][start:stop], do_aug[h][start:])
+                ds = (p * dp).astype(jnp.bfloat16)
+                dvs.append(nn(p.astype(jnp.bfloat16), do[start:]))
+                dks.append(nn(ds, q[start:]))
+                dqs.append(tn(ds, k[start:stop]))
+            dv_ref[pair, start:stop] = jnp.where(first, dvs[0], dvs[1]).astype(jnp.bfloat16)
+            dk_ref[pair, start:stop] = jnp.where(first, dks[0], dks[1]).astype(jnp.bfloat16)
+            dq = jnp.where(first, dqs[0], dqs[1])
+            if start == 0:
+                acc[...] = dq
+                if pair + 1 < group:
+                    ready = widen(pair + 1)
+            else:
+                acc[start:] += dq
+            dq_ref[pair, start:stop] = (acc[start:stop] * HD ** -0.5).astype(jnp.bfloat16)
+
+
+def heads(rows, offset):
+    return pl.BlockSpec((GROUP, rows, LANES), lambda slot, pair, lengths: (offset // GROUP + pair, slot, 0))
+
+
+def attention_forward(lengths, peaks, qkv):
+    slots = lengths.shape[0]
+    pairs, rows = qkv.shape[0] // 3, qkv.shape[1] // slots
+    return pl.pallas_call(
+        forward_kernel,
+        grid_spec=pltpu.PrefetchScalarGridSpec(
+            num_scalar_prefetch=1, grid=(slots, pairs // GROUP),
+            in_specs=[pl.BlockSpec(peaks.shape, lambda slot, pair, lengths: (0, 0, 0))] + [heads(rows, part * pairs) for part in range(3)],
+            out_specs=[heads(rows, 0)] * 2,
+            scratch_shapes=[pltpu.SMEM((1,), jnp.int32)]),
+        out_shape=[jax.ShapeDtypeStruct((pairs,) + qkv.shape[1:], jnp.bfloat16)] * 2,
+        compiler_params=pltpu.CompilerParams(vmem_limit_bytes=VMEM),
+        name="attention_forward",
+    )(lengths, peaks, qkv, qkv, qkv)
+
+
+def attention_backward(lengths, qkv, mixed, aux, d_mixed):
+    slots = lengths.shape[0]
+    pairs, rows = qkv.shape[0] // 3, qkv.shape[1] // slots
+    return pl.pallas_call(
+        backward_kernel,
+        grid_spec=pltpu.PrefetchScalarGridSpec(
+            num_scalar_prefetch=1, grid=(slots, pairs // GROUP),
+            in_specs=[heads(rows, part * pairs) for part in range(3)] + [heads(rows, 0)] * 3,
+            out_specs=[heads(rows, 0)] * 3,
+            scratch_shapes=[pltpu.VMEM((rows, LANES), jnp.float32)]),
+        out_shape=[jax.ShapeDtypeStruct((pairs,) + qkv.shape[1:], jnp.bfloat16)] * 3,
+        compiler_params=pltpu.CompilerParams(vmem_limit_bytes=VMEM),
+        name="attention_backward",
+    )(lengths, qkv, qkv, qkv, mixed, aux, d_mixed)
+
+
+def standardize(values):
+    centred = values - jnp.mean(values, axis=-1, keepdims=True)
+    inverse = lax.rsqrt(jnp.mean(centred * centred, axis=-1, keepdims=True) + epsilon)
+    return centred * inverse, inverse
+
+
+def pull_norm(grad, standard, inverse, gain):
+    scaled = grad * gain
+    centred = scaled - jnp.mean(scaled, axis=-1, keepdims=True)
+    return inverse * (centred - standard * jnp.mean(scaled * standard, axis=-1, keepdims=True))
+
+
+def f32(ref):
+    return ref[...].astype(jnp.float32)
+
+
+def pieces_of(rows, size):
+    return [slice(start, start + size) for start in range(0, rows, size)]
+
+
+def side_by_side(ref, part):
+    return jnp.concatenate([ref[pair, part] for pair in range(ref.shape[0])], axis=1)
+
+
+def spread(ref, part, values):
+    for pair in range(ref.shape[0]):
+        ref[pair, part] = values[:, pair * LANES:(pair + 1) * LANES].astype(ref.dtype)
+
+
+def fixed(shape):
+    return pl.BlockSpec(shape, lambda step: (0,) * len(shape), pipeline_mode=pl.Buffered(1))
+
+
+def sliding(depth):
+    return pl.BlockSpec((depth, TILE), lambda step: (0, step))
+
+
+def project_kernel(tokens, vectors, weight, downs, ups, qkv, lows, peaks, normed):
+    step = pl.program_id(0)
+    parts = pieces_of(tokens.shape[0], CHUNK)
+    lane = lax.broadcasted_iota(jnp.int32, (TILE, LANES), 0) // HD
+    each = jnp.where(lane == lax.broadcasted_iota(jnp.int32, (TILE, LANES), 1), 1.0, 0.0).astype(jnp.bfloat16)
+
+    @pl.when(step == 0)
+    def _():
+        for part in parts:
+            standard, _ = standardize(tokens[part].astype(jnp.float32))
+            normed[part] = (standard * vectors[GAIN:GAIN + 1] + vectors[SHIFT:SHIFT + 1]).astype(jnp.bfloat16)
+            lows[part] = nn(normed[part], downs[...]).astype(jnp.bfloat16)
+
+    for index, part in enumerate(parts):
+        values = (nn(normed[part], weight[...]) + vectors[pl.ds(JOINT + step, 1)] + nn(lows[part], ups[...])).astype(jnp.bfloat16)
+        spread(qkv, part, values)
+        peak = jnp.max(nn(values * values, each).reshape(-1, 8, LANES), axis=0)
+        peaks[0] = peak if index == 0 else jnp.maximum(peaks[0], peak)
+
+
+def project(tokens, vectors, weight, downs, ups):
+    rows, width = tokens.shape
+    wide, small = weight.shape[1], downs.shape[1]
+    return pl.pallas_call(
+        project_kernel,
+        grid=(wide // TILE,),
+        in_specs=[fixed((rows, width)), fixed(vectors.shape), sliding(width), fixed((width, small)), sliding(small)],
+        out_specs=[
+            pl.BlockSpec((TILE // LANES, rows, LANES), lambda step: (step, 0, 0)),
+            fixed((rows, small)),
+            pl.BlockSpec((1, 8, LANES), lambda step: (step, 0, 0)),
+        ],
+        out_shape=[
+            jax.ShapeDtypeStruct((wide // LANES, rows, LANES), jnp.bfloat16),
+            jax.ShapeDtypeStruct((rows, small), jnp.bfloat16),
+            jax.ShapeDtypeStruct((wide // TILE, 8, LANES), jnp.float32),
+        ],
+        scratch_shapes=[pltpu.VMEM((rows, width), jnp.bfloat16)],
+        compiler_params=pltpu.CompilerParams(vmem_limit_bytes=VMEM),
+        name="project",
+    )(tokens, vectors, weight, downs, ups)
+
+
+def gelu_and_slope(u):
+    c = (2.0 / jnp.pi) ** 0.5
+    square = u * u
+    share = 0.5 + 0.5 * jnp.tanh(u * (c + (c * 0.044715) * square))
+    value = u * share
+    slope = share + value * (1.0 - share) * (2 * c + (6 * c * 0.044715) * square)
+    return value, slope
+
+
+def feed_kernel(tokens, mixed, vectors, out_weight, up, down, result, middle, slopes, total, normed):
+    step = pl.program_id(0)
+    parts = pieces_of(tokens.shape[0], CHUNK)
+
+    @pl.when(step == 0)
+    def _():
+        for part in parts:
+            m = tokens[part].astype(jnp.float32) + nn(side_by_side(mixed, part), out_weight[...]) + vectors[OUT:OUT + 1]
+            middle[part] = m
+            standard, _ = standardize(m)
+            normed[part] = (standard * vectors[GAIN_TWO:GAIN_TWO + 1] + vectors[SHIFT_TWO:SHIFT_TWO + 1]).astype(jnp.bfloat16)
+            total[part] = m + vectors[DOWN:DOWN + 1]
+
+    for part in parts:
+        value, slope = gelu_and_slope(nn(normed[part], up[...]) + vectors[pl.ds(UP + step, 1)])
+        slopes[part] = slope.astype(jnp.bfloat16)
+        total[part] += nn(value.astype(jnp.bfloat16), down[...])
+
+    @pl.when(step == pl.num_programs(0) - 1)
+    def _():
+        result[...] = total[...].astype(jnp.bfloat16)
+
+
+def feed(tokens, mixed, vectors, out_weight, up, down):
+    rows, width = tokens.shape
+    wide = up.shape[1]
+    return pl.pallas_call(
+        feed_kernel,
+        grid=(wide // TILE,),
+        in_specs=[fixed((rows, width)), fixed(mixed.shape), fixed(vectors.shape), fixed((width, width)),
+                  sliding(width), pl.BlockSpec((TILE, width), lambda step: (step, 0))],
+        out_specs=[fixed((rows, width)), fixed((rows, width)), sliding(rows)],
+        out_shape=[
+            jax.ShapeDtypeStruct((rows, width), jnp.bfloat16),
+            jax.ShapeDtypeStruct((rows, width), jnp.float32),
+            jax.ShapeDtypeStruct((rows, wide), jnp.bfloat16),
+        ],
+        scratch_shapes=[pltpu.VMEM((rows, width), jnp.float32), pltpu.VMEM((rows, width), jnp.bfloat16)],
+        compiler_params=pltpu.CompilerParams(vmem_limit_bytes=VMEM),
+        name="feed",
+    )(tokens, mixed, vectors, out_weight, up, down)
+
+
+def feed_back_kernel(outer, slopes, up, down, middle, vectors, out_weight, d_middle, d_mixed, total):
+    step = pl.program_id(0)
+    parts = pieces_of(outer.shape[0], CHUNK)
+    for part in parts:
+        d_hidden = (nt(outer[part], down[...]) * slopes[part].astype(jnp.float32)).astype(jnp.bfloat16)
+        grad = nt(d_hidden, up[...])
+        total[part] = jnp.where(step == 0, grad, total[part] + grad)
+
+    @pl.when(step == pl.num_programs(0) - 1)
+    def _():
+        for part in parts:
+            standard, inverse = standardize(middle[part])
+            d = outer[part].astype(jnp.float32) + pull_norm(total[part], standard, inverse, vectors[GAIN_TWO:GAIN_TWO + 1])
+            d_middle[part] = d
+            spread(d_mixed, part, nt(d.astype(jnp.bfloat16), out_weight[...]))
+
+
+def feed_back(outer, slopes, up, down, middle, vectors, out_weight):
+    rows, width = outer.shape
+    wide = up.shape[1]
+    return pl.pallas_call(
+        feed_back_kernel,
+        grid=(wide // TILE,),
+        in_specs=[fixed((rows, width)), sliding(rows), sliding(width), pl.BlockSpec((TILE, width), lambda step: (step, 0)),
+                  fixed((rows, width)), fixed(vectors.shape), fixed((width, width))],
+        out_specs=[fixed((rows, width)), fixed((width // LANES, rows, LANES))],
+        out_shape=[jax.ShapeDtypeStruct((rows, width), jnp.float32), jax.ShapeDtypeStruct((width // LANES, rows, LANES), jnp.bfloat16)],
+        scratch_shapes=[pltpu.VMEM((rows, width), jnp.float32)],
+        compiler_params=pltpu.CompilerParams(vmem_limit_bytes=VMEM),
+        name="feed_back",
+    )(outer, slopes, up, down, middle, vectors, out_weight)
+
+
+def finish_kernel(dq, dk, dv, tokens, d_middle, lows, vectors, weight, downs, ups, grads, factors):
+    width = tokens.shape[1]
+    step = pl.program_id(0)
+    everything = slice(None)
+    d_queries, d_keys, d_values = (side_by_side(ref, everything) for ref in (dq, dk, dv))
+    standard, inverse = standardize(f32(tokens))
+    gain = vectors[GAIN:GAIN + 1]
+    normed = (standard * gain + vectors[SHIFT:SHIFT + 1]).astype(jnp.bfloat16)
+    small = (nt(d_queries, ups[:, :width]) + nt(d_values, ups[:, 2 * width:])).astype(jnp.bfloat16)
+    d_normed = nt(d_queries, weight[:, :width]) + nt(d_keys, weight[:, width:2 * width]) + nt(d_values, weight[:, 2 * width:]) + nt(small, downs[...])
+    grads[...] = (f32(d_middle) + pull_norm(d_normed, standard, inverse, gain)).astype(grads.dtype)
+    for index, part in enumerate((tn(small, normed), tn(lows[...], d_queries), tn(lows[...], d_values))):
+        factors[index] = jnp.where(step == 0, part, factors[index] + part)
+
+
+def finish(dq, dk, dv, tokens, d_middle, lows, vectors, weight, downs, ups):
+    rows, width = tokens.shape
+    small = downs.shape[1]
+    across = lambda span: pl.BlockSpec((CHUNK, span), lambda step: (step, 0))
+    paired = pl.BlockSpec((width // LANES, CHUNK, LANES), lambda step: (0, step, 0))
+    return pl.pallas_call(
+        finish_kernel,
+        grid=(rows // CHUNK,),
+        in_specs=[paired] * 3 + [across(width)] * 2 + [across(small), fixed(vectors.shape), fixed(weight.shape), fixed(downs.shape), fixed(ups.shape)],
+        out_specs=[across(width), fixed((3, small, width))],
+        out_shape=[jax.ShapeDtypeStruct((rows, width), jnp.bfloat16), jax.ShapeDtypeStruct((3, small, width), jnp.float32)],
+        compiler_params=pltpu.CompilerParams(vmem_limit_bytes=VMEM),
+        name="finish",
+    )(dq, dk, dv, tokens, d_middle, lows, vectors, weight, downs, ups)
+
+
+def sum_over(v, axis):
+    size = lax.axis_size(axis)
+    if size & (size - 1):
+        return lax.psum(v, axis)
+    step = 1
+    while step < size:
+        v = v + lax.ppermute(v, axis, [(i, i ^ step) for i in range(size)])
+        step *= 2
+    return v
+
+
+def whole_slots(
+    tokens,
+    lengths,
+    norm_gain,
+    norm_shift,
+    joint_weight,
+    query_bias,
+    value_bias,
+    output_weight,
+    output_bias,
+    second_gain,
+    second_shift,
+    upward_weight,
+    upward_bias,
+    down_weight,
+    down_bias,
+    query_down,
+    query_up,
+    value_down,
+    value_up,
+    cotangent,
+):
+    seqs_here, rows, width = tokens.shape
+    ranks = lax.axis_size("blk")
+    slots = seqs_here // ranks
+    adapter = 32.0 / RANK
+    positions = slots * rows * ranks
+
+    def to_slots(v):
+        pieces = lax.all_to_all(v.reshape(ranks, slots, rows, width), "blk", 0, 0, tiled=True)
+        return jnp.swapaxes(pieces, 0, 1).reshape(positions, width)
+
+    def to_rows(v):
+        pieces = jnp.swapaxes(v.reshape(slots, ranks, rows, width), 0, 1)
+        return lax.all_to_all(pieces, "blk", 0, 0, tiled=True).reshape(seqs_here, rows, width)
+
+    my_lengths = lax.dynamic_slice_in_dim(lengths, lax.axis_index("blk") * slots, slots)
+    vectors = jnp.concatenate(
+        (
+            norm_gain,
+            norm_shift,
+            query_bias,
+            jnp.zeros_like(query_bias),
+            value_bias,
+            output_bias,
+            second_gain,
+            second_shift,
+            down_bias,
+            upward_bias,
+        )
+    )
+    vectors = vectors.astype(jnp.float32).reshape(-1, width)
+    downs = jnp.pad(
+        jnp.concatenate((query_down, value_down), axis=1), ((0, 0), (0, LANES - 2 * RANK))
+    )
+    ups = adapter * (
+        jnp.pad(query_up, ((0, LANES - RANK), (0, 2 * width)))
+        + jnp.pad(value_up, ((RANK, LANES - 2 * RANK), (2 * width, 0)))
+    )
+    ups = ups.astype(jnp.bfloat16)
+    inner = to_slots(tokens)
+    cotangent, vectors, downs, ups, my_lengths = lax.optimization_barrier(
+        (cotangent, vectors, downs, ups, my_lengths)
+    )
+    outer = to_slots(cotangent)
+    qkv, lows, peaks = project(inner, vectors, joint_weight, downs, ups)
+    mixed, aux = attention_forward(my_lengths, peaks, qkv)
+    result, middle, slopes = feed(
+        inner, mixed, vectors, output_weight, upward_weight, down_weight
+    )
+    result, middle, slopes, outer = lax.optimization_barrier((result, middle, slopes, outer))
+    block_output = to_rows(result)
+    d_middle, d_mixed = feed_back(
+        outer, slopes, upward_weight, down_weight, middle, vectors, output_weight
+    )
+    d_queries, d_keys, d_values = attention_backward(
+        my_lengths, qkv, mixed, aux, d_mixed
+    )
+    grads, factors = finish(
+        d_queries,
+        d_keys,
+        d_values,
+        inner,
+        d_middle,
+        lows,
+        vectors,
+        joint_weight,
+        downs,
+        ups,
+    )
+    token_grads = to_rows(grads).astype(jnp.float32)
+    packed = jnp.concatenate(
+        (
+            factors[0, : 2 * RANK],
+            adapter * factors[1, :RANK],
+            adapter * factors[2, RANK : 2 * RANK],
+        )
+    )
+    packed = sum_over(sum_over(packed, "batch"), "blk")
+    query_down_grad, value_down_grad = packed[:RANK].T, packed[RANK : 2 * RANK].T
+    query_up_grad, value_up_grad = packed[2 * RANK : 3 * RANK], packed[3 * RANK :]
+    return (
+        block_output,
+        token_grads,
+        query_down_grad,
+        query_up_grad,
+        value_down_grad,
+        value_up_grad,
     )
 
 
@@ -223,6 +755,11 @@
     return (block_output, token_grads, sums[0], sums[1], sums[2], sums[3])
 
 
+def choose(tokens, *others):
+    fits = tokens.shape[0] % lax.axis_size("blk") == 0
+    return (whole_slots if fits else body)(tokens, *others)
+
+
 def solution(mesh):
     placed = (
         P("batch", "blk", None),
@@ -247,7 +784,7 @@
         P("batch", "blk", None),
     )
     return jax.shard_map(
-        body,
+        choose,
         mesh=mesh,
         in_specs=placed,
         out_specs=(P("batch", "blk", None), P("batch", "blk", None), P(), P(), P(), P()),

time: 1110 us -> 286 us (0.26)
  waiting for transfers between devices: 585 us -> 86.3 us
  matrix products: 288 us -> 0 us
  Pallas kernels: 0 us -> 151 us
  local copies, waits for them, and re-layouts: 144 us -> 7.65 us
  other arithmetic: 70.1 us -> 4.33 us
  starting transfers between devices: 0.16 us -> 30.8 us
  between operations: 14.6 us -> 1.14 us
    dot_general x25 -> x0, matrix products: 288 us -> none  [the longest x7 54.2 us: against(): lax.dot_general(left, right, (((1,), (1,)), ((), ())), preferred_element_...]
    reduce_scatter x1 -> x0, waiting for transfers between devices: 275 us -> none  [body(): lax.psum_scatter(stacked.astype(jnp.bfloat16), 'blk', scatter_dimension=0...]
    all_gather x2 -> x0, waiting for transfers between devices: 198 us -> none  [the longest x1 125 us: body(): key_piece = lax.all_gather(key_blocks, 'blk', axis=1, tiled=True)]
    pallas_call x0 -> x6, Pallas kernels: none -> 151 us  [the longest x1 36 us: attention_backward(): pl.pallas_call(backward_kernel, grid_spec=pltpu.PrefetchScalarGridSpec(nu...]
    psum x1 -> x0, waiting for transfers between devices: 111 us -> none  [body(): lax.psum((query_down_grad, query_up_grad, value_down_grad, value_up_grad)...]
    all_to_all x0 -> x4, waiting for transfers between devices: none -> 45.7 us  [the longest x2 45.7 us: to_slots(): lax.all_to_all(v.reshape(ranks, slots, rows, width), 'blk', 0, 0, tiled=T...]
    all_gather x2 -> x0, local copies, waits for them, and re-layouts: 43.8 us -> none  [the longest x1 22.3 us: body(): key_piece = lax.all_gather(key_blocks, 'blk', axis=1, tiled=True)]
    another operation x2 -> x0, local copies, waits for them, and re-layouts: 43.1 us -> none  [body(): jnp.stack((d_keys_all.reshape(length_all, seqs_here, width), d_values_all...]
  transfers between devices with their start and end apart: 4 -> 9, of which waited for: 4 -> 6; matrix products, arithmetic and copies ran while one was open for 14% -> 2% of each run, Pallas kernels for 0% -> 54%
where the time goes in v3:
time: 286 us; the launch traced here: 282 us
  Pallas kernels  151 us (53%)
  waiting for transfers between devices  86.3 us (30%)
  starting transfers between devices  30.8 us (11%)
  local copies, waits for them, and re-layouts  7.65 us (3%)
  other arithmetic  4.33 us (2%)
    all_to_all x2, waiting for transfers between devices, to_slots(): lax.all_to_all(v.reshape(ranks, slots, rows, width), 'blk', 0, 0, tiled=T...  45.7 us
    ppermute x5, waiting for transfers between devices, sum_over(): v = v + lax.ppermute(v, axis, [(i, i ^ step) for i in range(size)])  40.6 us
    pallas_call x1, Pallas kernels, attention_backward(): pl.pallas_call(backward_kernel, grid_spec=pltpu.PrefetchScalarGridSpec(nu...  36 us
    pallas_call x1, Pallas kernels, feed(): pl.pallas_call(feed_kernel, grid=(wide // TILE,), in_specs=[fixed((rows,...  33.5 us
    pallas_call x1, Pallas kernels, feed_back(): pl.pallas_call(feed_back_kernel, grid=(wide // TILE,), in_specs=[fixed((r...  30.8 us
    pallas_call x1, Pallas kernels, finish(): pl.pallas_call(finish_kernel, grid=(rows // CHUNK,), in_specs=[paired] *...  17.4 us
    pallas_call x1, Pallas kernels, attention_forward(): pl.pallas_call(forward_kernel, grid_spec=pltpu.PrefetchScalarGridSpec(num...  17 us
    pallas_call x1, Pallas kernels, project(): pl.pallas_call(project_kernel, grid=(wide // TILE,), in_specs=[fixed((row...  16.5 us
  transfers between devices with their start and end apart: 9, of which 6 were waited for; matrix products, arithmetic and copies ran while one was open for 2% of the time, Pallas kernels for 54%

profile of v3, /device:TPU:0, one launch (start us, length us, event | category | flops | bytes accessed | tf_op | source)
XLA Modules:
  0.0 281.5 jit_solution(1146899629538912263)
XLA Ops:
  0.8 6.5 %all-to-all-start = ((bf16[8,1,128,1024]{3,2,1,0:T(8,128)(2,1)}), bf16[8,1,128,1024]{3,2,1,0:T(8,128)(2,1)S(1)}, u32[]{:S(2)}, u32[]{:S(2)}) async-start(bf16[8,1,128,1024]{3,2,1,0:T(8,128)(2,1)} %bitcast.28), calls=%async_computation | async-start | bytes 4194304 | tf_op jit(solution)/shard_map/all_to_all | solution.py:491
  7.5 0.7 reshape.35.vectors
  8.1 0.2 copy.28
  8.3 0.6 dynamic_slice.3.lengths
  8.9 0.7 pad.12.downs
  9.7 1.0 add_multiply_fusion.ups
  10.7 45.7 %all-to-all-done = bf16[8,1,128,1024]{3,2,1,0:T(8,128)(2,1)S(1)} async-done(((bf16[8,1,128,1024]{3,2,1,0:T(8,128)(2,1)}), bf16[8,1,128,1024]{3,2,1,0:T(8,128)(2,1)S(1)}, u32[]{:S(2)}, u32[]{:S(2)}) %all-to-all-start) | async-done | bytes 2097184 | tf_op jit(solution)/shard_map/all_to_all | solution.py:491
  56.3 1.3 copy-done
  57.6 4.4 %all-to-all-start.1 = ((bf16[8,1,128,1024]{3,2,1,0:T(8,128)(2,1)}), bf16[8,1,128,1024]{3,2,1,0:T(8,128)(2,1)}, u32[]{:S(2)}, u32[]{:S(2)}) async-start(bf16[8,1,128,1024]{3,2,1,0:T(8,128)(2,1)} %bitcast.29), calls=%async_computation.1 | async-start | bytes 4194304 | tf_op jit(solution)/shard_map/all_to_all | solution.py:491
  62.0 16.5 %project.1 = (bf16[24,1024,128]{2,1,0:T(8,128)(2,1)}, bf16[1024,128]{1,0:T(8,128)(2,1)}, f32[3,8,128]{2,1,0:T(8,128)}) custom-call(bf16[1024,1024]{1,0:T(8,128)(2,1)} %bitcast.24, f32[13,1024]{1,0:T(8,128)} %reshape.35.vectors, bf16[1024,3072]{1,0:T(8,128)(2,1)} %weight.3, bf16[1024,128]{1,0:T(8,128)(2,1)} %pad.12.downs, bf16[128,3072]{1,0:T(8,128)(2,1)} %add_multiply_fusion.ups), custom_call_target="tpu_custom_call" | custom-call | tf_op jit(solution)/shard_map/project/pallas_call | solution.py:315
  78.5 17.0 %attention_forward.1 = (bf16[8,1024,128]{2,1,0:T(8,128)(2,1)}, bf16[8,1024,128]{2,1,0:T(8,128)(2,1)}) custom-call(s32[1]{0:T(128)} %dynamic_slice.3.lengths, f32[3,8,128]{2,1,0:T(8,128)} %get-tuple-element.34.peaks, bf16[24,1024,128]{2,1,0:T(8,128)(2,1)} %get-tuple-element.35.q_ref.k_ref.v_ref, bf16[24,1024,128]{2,1,0:T(8,128)(2,1)} %get-tuple-element.35.q_ref.k_ref.v_ref, ...), custom_call_target="tpu_custom_call" | custom-call | tf_op jit(solution)/shard_map/attention_forward/pallas_call | solution.py:226
  95.5 33.5 %feed.1 = (bf16[1024,1024]{1,0:T(8,128)(2,1)}, f32[1024,1024]{1,0:T(8,128)}, bf16[1024,4096]{1,0:T(8,128)(2,1)}) custom-call(bf16[1024,1024]{1,0:T(8,128)(2,1)} %bitcast.25, bf16[8,1024,128]{2,1,0:T(8,128)(2,1)} %get-tuple-element.36.mixed.mixed_ref, f32[13,1024]{1,0:T(8,128)} %reshape.35.vectors, bf16[1024,1024]{1,0:T(8,128)(2,1)} %out_weight.3, ...), custom_call_target="tpu_custom_call" | custom-call | tf_op jit(solution)/shard_map/feed/pallas_call | solution.py:370
  129.1 5.3 %all-to-all-start.2 = ((bf16[8,1,128,1024]{3,2,1,0:T(8,128)(2,1)}), bf16[8,1,128,1024]{3,2,1,0:T(8,128)(2,1)S(1)}, u32[]{:S(2)}, u32[]{:S(2)}) async-start(bf16[8,1,128,1024]{3,2,1,0:T(8,128)(2,1)} %bitcast.31), calls=%async_computation.2 | async-start | bytes 4194304 | tf_op jit(solution)/shard_map/all_to_all | solution.py:496
  134.4 30.8 %feed_back.1 = (f32[1024,1024]{1,0:T(8,128)}, bf16[8,1024,128]{2,1,0:T(8,128)(2,1)}) custom-call(bf16[1024,1024]{1,0:T(8,128)(2,1)} %bitcast.3.outer, bf16[1024,4096]{1,0:T(8,128)(2,1)} %get-tuple-element.44.slopes, bf16[1024,4096]{1,0:T(8,128)(2,1)} %up.3, bf16[4096,1024]{1,0:T(8,128)(2,1)} %down.3, f32[1024,1024]{1,0:T(8,128)} %get-tuple-element.45.middle, ...), custom_call_target="tpu_custom_call" | custom-call | tf_op jit(solution)/shard_map/feed_back/pallas_call | solution.py:407
  165.2 36.0 %attention_backward.1 = (bf16[8,1024,128]{2,1,0:T(8,128)(2,1)}, bf16[8,1024,128]{2,1,0:T(8,128)(2,1)}, bf16[8,1024,128]{2,1,0:T(8,128)(2,1)}) custom-call(s32[1]{0:T(128)} %dynamic_slice.3.lengths, bf16[24,1024,128]{2,1,0:T(8,128)(2,1)} %get-tuple-element.35.q_ref.k_ref.v_ref, bf16[24,1024,128]{2,1,0:T(8,128)(2,1)} %get-tuple-element.35.q_ref.k_ref.v_ref, ...), custom_call_target="tpu_custom_call" | custom-call | tf_op jit(solution)/shard_map/attention_backward/pallas_call | solution.py:242
  201.2 17.4 %finish.1 = (bf16[1024,1024]{1,0:T(8,128)(2,1)}, f32[3,128,1024]{2,1,0:T(8,128)}) custom-call(bf16[8,1024,128]{2,1,0:T(8,128)(2,1)} %get-tuple-element.47.dq, bf16[8,1024,128]{2,1,0:T(8,128)(2,1)} %get-tuple-element.48.dk, bf16[8,1024,128]{2,1,0:T(8,128)(2,1)} %get-tuple-element.49.dv, bf16[1024,1024]{1,0:T(8,128)(2,1)} %bitcast.26, ...), custom_call_target="tpu_custom_call" | custom-call | tf_op jit(solution)/shard_map/finish/pallas_call | solution.py:440
  218.6 1.3 copy-done.1
  219.9 5.1 %all-to-all-start.3 = ((bf16[8,1,128,1024]{3,2,1,0:T(8,128)(2,1)}), bf16[8,1,128,1024]{3,2,1,0:T(8,128)(2,1)S(1)}, u32[]{:S(2)}, u32[]{:S(2)}) async-start(bf16[8,1,128,1024]{3,2,1,0:T(8,128)(2,1)} %bitcast.30), calls=%async_computation.3 | async-start | bytes 4194304 | tf_op jit(solution)/shard_map/all_to_all | solution.py:496
  225.0 0.8 slice_bitcast_fusion
  225.8 0.8 multiply_bitcast_fusion.1
  226.6 1.6 collective-permute-start
  228.1 3.0 %collective-permute-done = f32[16,1024]{1,0:T(8,128)S(1)} collective-permute-done((f32[16,1024]{1,0:T(8,128)S(1)}, f32[16,1024]{1,0:T(8,128)S(1)}, u32[]{:S(2)}, u32[]{:S(2)}) %collective-permute-start) | collective-permute-done | bytes 65568 | tf_op jit(solution)/shard_map/ppermute | solution.py:457
  231.2 1.6 collective-permute-start.1
  232.7 2.8 collective-permute-done.1
  235.6 1.2 collective-permute-done.2
  236.8 1.8 collective-permute-start.3
  238.7 22.6 %collective-permute-done.3 = f32[16,1024]{1,0:T(8,128)S(1)} collective-permute-done((f32[16,1024]{1,0:T(8,128)S(1)}, f32[16,1024]{1,0:T(8,128)S(1)}, u32[]{:S(2)}, u32[]{:S(2)}) %collective-permute-start.3) | collective-permute-done | bytes 65568 | tf_op jit(solution)/shard_map/ppermute | solution.py:457
  261.3 4.6 %collective-permute-start.4 = (f32[16,1024]{1,0:T(8,128)S(1)}, f32[16,1024]{1,0:T(8,128)S(1)}, u32[]{:S(2)}, u32[]{:S(2)}) collective-permute-start(f32[16,1024]{1,0:T(8,128)S(1)} %add.32), channel_id=1, source_target_pairs={{0,4},{1,5},{2,6},{3,7},{4,0},{5,1},{6,2},{7,3},{8,12},{9,13},{10,... | collective-permute-start | bytes 196616 | tf_op jit(solution)/shard_map/ppermute | solution.py:457
  265.9 11.0 %collective-permute-done.4 = f32[16,1024]{1,0:T(8,128)S(1)} collective-permute-done((f32[16,1024]{1,0:T(8,128)S(1)}, f32[16,1024]{1,0:T(8,128)S(1)}, u32[]{:S(2)}, u32[]{:S(2)}) %collective-permute-start.4) | collective-permute-done | bytes 65568 | tf_op jit(solution)/shard_map/ppermute | solution.py:457
  276.9 0.6 fusion.1
  277.5 2.5 bitcast_convert_fusion
  280.0 1.3 copy.41
  (53 shorter events, 0.3 us)
Async XLA Ops:
  0.6 6.6 %copy-start.8 = (bf16[1024]{0:T(1024)(128)(2,1)S(1)}, bf16[1024]{0:T(1024)(128)(2,1)}, u32[]{:S(2)}) copy-start(bf16[1024]{0:T(1024)(128)(2,1)} %param.22) | copy-start | bytes 6148
  0.6 6.6 %copy-start.9 = (bf16[1024]{0:T(1024)(128)(2,1)S(1)}, bf16[1024]{0:T(1024)(128)(2,1)}, u32[]{:S(2)}) copy-start(bf16[1024]{0:T(1024)(128)(2,1)} %param.23) | copy-start | bytes 6148
  0.7 6.6 %copy-start.10 = (bf16[1024]{0:T(1024)(128)(2,1)S(1)}, bf16[1024]{0:T(1024)(128)(2,1)}, u32[]{:S(2)}) copy-start(bf16[1024]{0:T(1024)(128)(2,1)} %param.25) | copy-start | bytes 6148
  0.7 6.7 %copy-start.11 = (bf16[1024]{0:T(1024)(128)(2,1)S(1)}, bf16[1024]{0:T(1024)(128)(2,1)}, u32[]{:S(2)}) copy-start(bf16[1024]{0:T(1024)(128)(2,1)} %param.26) | copy-start | bytes 6148
  0.7 6.7 %copy-start.12 = (bf16[1024]{0:T(1024)(128)(2,1)S(1)}, bf16[1024]{0:T(1024)(128)(2,1)}, u32[]{:S(2)}) copy-start(bf16[1024]{0:T(1024)(128)(2,1)} %param.28) | copy-start | bytes 6148
  0.7 6.7 %copy-start.13 = (bf16[1024]{0:T(1024)(128)(2,1)S(1)}, bf16[1024]{0:T(1024)(128)(2,1)}, u32[]{:S(2)}) copy-start(bf16[1024]{0:T(1024)(128)(2,1)} %param.29) | copy-start | bytes 6148
  0.7 6.7 %copy-start.14 = (bf16[1024]{0:T(1024)(128)(2,1)S(1)}, bf16[1024]{0:T(1024)(128)(2,1)}, u32[]{:S(2)}) copy-start(bf16[1024]{0:T(1024)(128)(2,1)} %param.30) | copy-start | bytes 6148
  0.7 6.7 %copy-start.15 = (bf16[1024]{0:T(1024)(128)(2,1)S(1)}, bf16[1024]{0:T(1024)(128)(2,1)}, u32[]{:S(2)}) copy-start(bf16[1024]{0:T(1024)(128)(2,1)} %param.34) | copy-start | bytes 6148
  0.7 6.7 %copy-start.5 = (bf16[4096]{0:T(1024)(128)(2,1)S(1)}, bf16[4096]{0:T(1024)(128)(2,1)}, u32[]{:S(2)}) copy-start(bf16[4096]{0:T(1024)(128)(2,1)} %param.32) | copy-start | bytes 24580
  0.7 7.4 %copy-start.6 = (bf16[1024,4]{0,1:T(4,128)(2,1)S(1)}, bf16[1024,4]{0,1:T(4,128)(2,1)}, u32[]{:S(2)}) copy-start(bf16[1024,4]{0,1:T(4,128)(2,1)} %param.37) | copy-start | bytes 24580
  0.7 7.4 %copy-start.7 = (bf16[1024,4]{0,1:T(4,128)(2,1)S(1)}, bf16[1024,4]{0,1:T(4,128)(2,1)}, u32[]{:S(2)}) copy-start(bf16[1024,4]{0,1:T(4,128)(2,1)} %param.35) | copy-start | bytes 24580
  0.7 7.6 %copy-start.16 = (s32[8]{0:T(128)S(1)}, s32[8]{0:T(128)}, u32[]{:S(2)}) copy-start(s32[8]{0:T(128)} %param.21) | copy-start | bytes 100
  0.8 8.9 %copy-start.3 = (bf16[4,1024]{1,0:T(4,128)(2,1)S(1)}, bf16[4,1024]{1,0:T(4,128)(2,1)}, u32[]{:S(2)}) copy-start(bf16[4,1024]{1,0:T(4,128)(2,1)} %param.38) | copy-start | bytes 24580
  0.8 8.9 %copy-start.4 = (bf16[4,1024]{1,0:T(4,128)(2,1)S(1)}, bf16[4,1024]{1,0:T(4,128)(2,1)}, u32[]{:S(2)}) copy-start(bf16[4,1024]{1,0:T(4,128)(2,1)} %param.36) | copy-start | bytes 24580
  0.8 55.5 %all-to-all-start = ((bf16[8,1,128,1024]{3,2,1,0:T(8,128)(2,1)}), bf16[8,1,128,1024]{3,2,1,0:T(8,128)(2,1)S(1)}, u32[]{:S(2)}, u32[]{:S(2)}) async-start(bf16[8,1,128,1024]{3,2,1,0:T(8,128)(2,1)} %bitcast.28), calls=%async_computation | async-start | bytes 4194304 | tf_op jit(solution)/shard_map/all_to_all | solution.py:491
  56.3 1.3 copy-start
  57.6 71.4 %all-to-all-start.1 = ((bf16[8,1,128,1024]{3,2,1,0:T(8,128)(2,1)}), bf16[8,1,128,1024]{3,2,1,0:T(8,128)(2,1)}, u32[]{:S(2)}, u32[]{:S(2)}) async-start(bf16[8,1,128,1024]{3,2,1,0:T(8,128)(2,1)} %bitcast.29), calls=%async_computation.1 | async-start | bytes 4194304 | tf_op jit(solution)/shard_map/all_to_all | solution.py:491
  129.1 89.5 %all-to-all-start.2 = ((bf16[8,1,128,1024]{3,2,1,0:T(8,128)(2,1)}), bf16[8,1,128,1024]{3,2,1,0:T(8,128)(2,1)S(1)}, u32[]{:S(2)}, u32[]{:S(2)}) async-start(bf16[8,1,128,1024]{3,2,1,0:T(8,128)(2,1)} %bitcast.31), calls=%async_computation.2 | async-start | bytes 4194304 | tf_op jit(solution)/shard_map/all_to_all | solution.py:496
  218.6 1.3 copy-start.1
  219.9 57.6 %all-to-all-start.3 = ((bf16[8,1,128,1024]{3,2,1,0:T(8,128)(2,1)}), bf16[8,1,128,1024]{3,2,1,0:T(8,128)(2,1)S(1)}, u32[]{:S(2)}, u32[]{:S(2)}) async-start(bf16[8,1,128,1024]{3,2,1,0:T(8,128)(2,1)} %bitcast.30), calls=%async_computation.3 | async-start | bytes 4194304 | tf_op jit(solution)/shard_map/all_to_all | solution.py:496
  226.6 4.6 %collective-permute-start = (f32[16,1024]{1,0:T(8,128)S(1)}, f32[16,1024]{1,0:T(8,128)S(1)}, u32[]{:S(2)}, u32[]{:S(2)}) collective-permute-start(f32[16,1024]{1,0:T(8,128)S(1)} %pad_maximum_fusion), channel_id=1, source_target_pairs={{0,8},{8,0},{16,24},{24,16},{1,9},{9,1},{17,25},{25,17},{2,10},{10... | collective-permute-start | bytes 196616 | tf_op jit(solution)/shard_map/ppermute | solution.py:457
  231.2 4.3 %collective-permute-start.1 = (f32[16,1024]{1,0:T(8,128)S(1)}, f32[16,1024]{1,0:T(8,128)S(1)}, u32[]{:S(2)}, u32[]{:S(2)}) collective-permute-start(f32[16,1024]{1,0:T(8,128)S(1)} %fusion), channel_id=1, source_target_pairs={{0,16},{8,24},{16,0},{24,8},{1,17},{9,25},{17,1},{25,9},{2,18},{10... | collective-permute-start | bytes 196616 | tf_op jit(solution)/shard_map/ppermute | solution.py:457
  235.5 1.3 collective-permute-start.2
  236.8 24.4 %collective-permute-start.3 = (f32[16,1024]{1,0:T(8,128)S(1)}, f32[16,1024]{1,0:T(8,128)S(1)}, u32[]{:S(2)}, u32[]{:S(2)}) collective-permute-start(f32[16,1024]{1,0:T(8,128)S(1)} %add.31), channel_id=1, source_target_pairs={{0,2},{1,3},{2,0},{3,1},{4,6},{5,7},{6,4},{7,5},{8,10},{9,11},{10,... | collective-permute-start | bytes 196616 | tf_op jit(solution)/shard_map/ppermute | solution.py:457
  261.3 15.6 %collective-permute-start.4 = (f32[16,1024]{1,0:T(8,128)S(1)}, f32[16,1024]{1,0:T(8,128)S(1)}, u32[]{:S(2)}, u32[]{:S(2)}) collective-permute-start(f32[16,1024]{1,0:T(8,128)S(1)} %add.32), channel_id=1, source_target_pairs={{0,4},{1,5},{2,6},{3,7},{4,0},{5,1},{6,2},{7,3},{8,12},{9,13},{10,... | collective-permute-start | bytes 196616 | tf_op jit(solution)/shard_map/ppermute | solution.py:457
  277.5 2.5 copy-start.2
